TPU v7x, 32 devices: a whole 2x2x4 slice. The times are simulated.
32 devices in a mesh: section: 4 (over y, x), adapter: 2 (over core), mp: 4 (over z).
Axes of the slice: x: 2, y: 2, z: 4, core: 2. Of those that a mesh axis runs over, the one named last changes fastest.
Arguments:
- forward_input: bfloat16 [4, 2048, 8192], P('section', 'adapter', 'mp'), may hold values from -6 to 6
- stored_input: bfloat16 [4, 2048, 8192], P('section', 'adapter', 'mp'), may hold values from -6 to 6
- output_gradient: bfloat16 [4, 2048, 8192], P('section', 'adapter', 'mp'), may hold values from -6 to 6
- frozen_weight: bfloat16 [4, 8192, 8192], P('section', None, 'mp'), may hold values from -0.0625 to 0.0625
- adapter_down_factor: bfloat16 [4, 16, 64, 8192], P('section', 'adapter', None, 'mp'), may hold values from -0.0625 to 0.0625
- adapter_up_factor: bfloat16 [4, 16, 64, 8192], P('section', 'adapter', None, 'mp'), may hold values from -0.0625 to 0.0625
- adapter_index_list: int32 [2, 4, 16], P(None, 'section', 'adapter'), may hold values from 0 to 15, as said below
Outputs:
- fwd_out: bfloat16 [4, 2048, 8192], P('section', 'adapter', 'mp')
- grad_in: bfloat16 [4, 2048, 8192], P('section', 'adapter', 'mp')
- grad_a: bfloat16 [4, 16, 64, 8192], P('section', 'adapter', None, 'mp')
- grad_b: bfloat16 [4, 16, 64, 8192], P('section', 'adapter', None, 'mp')
Inputs may be any that keep to these rules, and one draw needn't show every extreme that they name: `adapter_index_list`: owner o holds adapters o * 8 to (o + 1) * 8 - 1. Of the 8 sequences of one index of the adapter axis, for one segment and one micro-batch, at most 5 use adapters of one owner; for each segment and micro-batch one owner gets exactly 5 from every index.
All inputs are finite; a program needn't handle non-finite values.
Results may differ from a plain program's by a relative error of at most 0.013.
Values may be sent and summed in bfloat16 or wider, within the bound.
A program may use at most 192 MiB of HBM per device.

v0:
```python
import jax
import jax.numpy as jnp
from jax import lax
from jax.sharding import PartitionSpec as P

adapter_scale = 2.0


def shifted(value, axis, steps):
    count = lax.axis_size(axis)
    pairs = [(source, (source + steps) % count) for source in range(count)]
    return lax.ppermute(value, axis, pairs)


def pack_slots(ids_row, capacity, owners_count, adapters_held):
    seq_count = ids_row.shape[0]
    owners = ids_row // adapters_held
    positions = jnp.arange(seq_count, dtype=jnp.int32)
    same_owner = owners[:, None] == owners[None, :]
    earlier = positions[None, :] < positions[:, None]
    slot_rank = jnp.sum((same_owner & earlier).astype(jnp.int32), axis=1)
    slot_index = owners * capacity + slot_rank
    slot_ids = jnp.arange(owners_count * capacity, dtype=jnp.int32)
    placing = (slot_index[None, :] == slot_ids[:, None]).astype(jnp.bfloat16)
    local_ids = ids_row % adapters_held
    pick_seq = (local_ids[:, None] == jnp.arange(adapters_held, dtype=jnp.int32)[None, :]).astype(
        jnp.bfloat16
    )
    chosen = jnp.dot(placing, pick_seq, preferred_element_type=jnp.float32).astype(jnp.bfloat16)
    return (placing, chosen.reshape(owners_count, capacity, adapters_held))


def select_slabs(chosen, table):
    return jnp.einsum("nkj,jrm->nkrm", chosen, table, preferred_element_type=jnp.float32).astype(
        jnp.bfloat16
    )


def local(
    forward_input,
    stored_input,
    output_gradient,
    frozen_weight,
    adapter_down_factor,
    adapter_up_factor,
    adapter_index_list,
):
    single_float = jnp.float32
    brain_half_float = jnp.bfloat16
    highest_accuracy = lax.Precision.HIGHEST
    owners_count = lax.axis_size("adapter")
    seq_count = adapter_index_list.shape[2]
    capacity = max(2, seq_count // owners_count + 1)
    slot_total = owners_count * capacity
    hidden_state = forward_input[0]
    saved = stored_input[0]
    cotangent = output_gradient[0]
    weight = frozen_weight[0]
    down_factor_table = adapter_down_factor[0]
    up_factor_table = adapter_up_factor[0]
    adapters_held = down_factor_table.shape[0]
    rows, width = hidden_state.shape
    seq_len = rows // seq_count
    forward_base_output = jnp.dot(
        lax.all_gather(hidden_state, "mp", axis=1, tiled=True),
        weight,
        preferred_element_type=single_float,
    )
    back_term = lax.dot_general(
        cotangent, weight, (((1,), (1,)), ((), ())), preferred_element_type=single_float
    )
    base_back = lax.psum_scatter(
        back_term.astype(jnp.bfloat16), "mp", scatter_dimension=1, tiled=True
    ).astype(jnp.float32)
    forward_placement, pick_fwd = pack_slots(
        adapter_index_list[0, 0], capacity, owners_count, adapters_held
    )
    placing_back, pick_back = pack_slots(
        adapter_index_list[1, 0], capacity, owners_count, adapters_held
    )

    def to_slots(placing, values):
        flat_rows = values.reshape(seq_count, seq_len * width)
        packed = jnp.dot(placing, flat_rows, preferred_element_type=single_float).astype(
            brain_half_float
        )
        return packed.reshape(owners_count, capacity, seq_len, width)

    def slots_gathered(placing, values):
        flat_rows = values.reshape(slot_total, seq_len * width)
        spread = lax.dot_general(
            placing, flat_rows, (((0,), (0,)), ((), ())), preferred_element_type=single_float
        )
        return spread.reshape(rows, width)

    send_fwd = to_slots(forward_placement, hidden_state)
    send_saved = to_slots(placing_back, saved)
    send_grad = to_slots(placing_back, cotangent)
    rows_fwd = lax.all_to_all(send_fwd, "adapter", split_axis=0, concat_axis=0, tiled=True)
    rows_saved = lax.all_to_all(send_saved, "adapter", split_axis=0, concat_axis=0, tiled=True)
    token_row_gradient = lax.all_to_all(
        send_grad, "adapter", split_axis=0, concat_axis=0, tiled=True
    )
    owner_fwd = lax.all_to_all(pick_fwd, "adapter", split_axis=0, concat_axis=0, tiled=True)
    owner_back = lax.all_to_all(pick_back, "adapter", split_axis=0, concat_axis=0, tiled=True)
    first_fwd = select_slabs(owner_fwd, down_factor_table)
    second_fwd = select_slabs(owner_fwd, up_factor_table)
    first_back = select_slabs(owner_back, down_factor_table)
    second_back = select_slabs(owner_back, up_factor_table)
    rank_fwd = jnp.einsum(
        "nklm,nkrm->nkrl", rows_fwd, first_fwd, preferred_element_type=single_float
    )
    rank_back = jnp.einsum(
        "nklm,nkrm->nkrl", rows_saved, first_back, preferred_element_type=single_float
    )
    rank_space_gradient = jnp.einsum(
        "nklm,nkrm->nkrl", token_row_gradient, second_back, preferred_element_type=single_float
    )
    rank_fwd, rank_back, rank_space_gradient = lax.psum(
        (rank_fwd, rank_back, rank_space_gradient), "mp"
    )
    coded_fwd = rank_fwd.astype(brain_half_float)
    encoded_backward = rank_back.astype(brain_half_float)
    gradient_scaled = (adapter_scale * rank_space_gradient).astype(brain_half_float)
    adapter_token_rows = jnp.einsum(
        "nkrl,nkrm->nklm", coded_fwd, second_fwd, preferred_element_type=single_float
    ).astype(brain_half_float)
    back_rows = jnp.einsum(
        "nkrl,nkrm->nklm", gradient_scaled, first_back, preferred_element_type=single_float
    ).astype(brain_half_float)
    adapter_home_output = lax.all_to_all(
        adapter_token_rows, "adapter", split_axis=0, concat_axis=0, tiled=True
    )
    returned_home = lax.all_to_all(back_rows, "adapter", split_axis=0, concat_axis=0, tiled=True)
    slot_down_gradient = jnp.einsum(
        "nkrl,nklm->nkrm", gradient_scaled, rows_saved, preferred_element_type=single_float
    )
    slot_up_gradient = adapter_scale * jnp.einsum(
        "nkrl,nklm->nkrm", encoded_backward, token_row_gradient, preferred_element_type=single_float
    )
    adapter_home_output, returned_home, slot_down_gradient, slot_up_gradient, owner_selection = (
        adapter_home_output,
        returned_home,
        slot_down_gradient,
        slot_up_gradient,
        owner_back,
    )
    owner_weights = owner_selection.astype(single_float)
    grad_a = (
        jnp.einsum("nkj,nkrm->jrm", owner_weights, slot_down_gradient, precision=highest_accuracy)
        / seq_len
    ).astype(brain_half_float)
    grad_b = (
        jnp.einsum("nkj,nkrm->jrm", owner_weights, slot_up_gradient, precision=highest_accuracy)
        / seq_len
    ).astype(brain_half_float)
    adapter_sequence_output = slots_gathered(forward_placement, adapter_home_output)
    back_seq = slots_gathered(placing_back, returned_home)
    forward_output = (
        hidden_state.astype(single_float)
        + forward_base_output
        + adapter_scale * adapter_sequence_output
    ).astype(brain_half_float)
    out_back = (cotangent.astype(single_float) + base_back + back_seq).astype(brain_half_float)
    fwd_next = shifted(forward_output, "section", 1)
    back_next = shifted(out_back, "section", -1)
    return (fwd_next[None], back_next[None], grad_a[None], grad_b[None])


def solution(mesh):
    in_specs = (
        P("section", "adapter", "mp"),
        P("section", "adapter", "mp"),
        P("section", "adapter", "mp"),
        P("section", None, "mp"),
        P("section", "adapter", None, "mp"),
        P("section", "adapter", None, "mp"),
        P(None, "section", "adapter"),
    )
    out_specs = (
        P("section", "adapter", "mp"),
        P("section", "adapter", "mp"),
        P("section", "adapter", None, "mp"),
        P("section", "adapter", None, "mp"),
    )
    return jax.shard_map(local, mesh=mesh, in_specs=in_specs, out_specs=out_specs, check_vma=False)
```

profile of v0, /device:TPU:18, one launch (start us, length us, event | category | flops | bytes accessed | tf_op | source)
XLA Modules:
  0.0 806.2 jit_solution(9370106061831690532)
XLA Ops:
  19.1 7.7 convolution_convert_fusion.1
  26.8 11.2 %copy.96 = bf16[2,8,128,2048]{3,2,1,0:T(8,128)(2,1)} copy(bf16[2,8,128,2048]{3,1,2,0:T(8,128)(2,1)} %bitcast.139) | data formatting | bytes 16777216
  55.2 7.5 fusion.31
  63.5 42.4 %fusion.5 = bf16[1024,8192]{1,0:T(8,128)(2,1)} fusion(bf16[1,8192,2048]{2,1,0:T(8,128)(2,1)} %param.10, bf16[1,1024,2048]{2,1,0:T(8,128)(2,1)} %param.9), kind=kOutput, calls=%fused_computation.9 | convolution fusion | flops 34368126976 | bytes 54525952 | tf_op jit(solution)/shard_map/dot_general | solution.py:69
  105.9 6.3 reshape_squeeze.11
  112.2 8.8 %convolution_convert_fusion = bf16[10,262144]{1,0:T(8,128)(2,1)} fusion(bf16[8,262144]{1,0:T(8,128)(2,1)} %reshape_squeeze.11, s32[8]{0:T(128)S(1)} %multiply_add_fusion), kind=kOutput, calls=%fused_computation | convolution fusion | flops 44564560 | bytes 9437216 | tf_op jit(solution)/shard_map/dot_general | solution.py:84
  121.0 11.4 %copy.98 = bf16[2,8,128,2048]{3,2,1,0:T(8,128)(2,1)} copy(bf16[2,8,128,2048]{3,1,2,0:T(8,128)(2,1)} %bitcast.140) | data formatting | bytes 16777216
  158.4 6.9 fusion.68
  170.8 11.3 %copy.94 = bf16[2,8,128,2048]{3,2,1,0:T(8,128)(2,1)} copy(bf16[2,8,128,2048]{3,1,2,0:T(8,128)(2,1)} %bitcast.141) | data formatting | bytes 16777216
  199.3 6.7 fusion.34
  206.0 65.3 %all-reduce.5 = (bf16[2,5,64,128]{3,2,1,0:T(8,128)(2,1)S(1)}, bf16[2,5,64,128]{3,2,1,0:T(8,128)(2,1)S(1)}) all-reduce(f32[2,5,64,128]{3,2,1,0:T(8,128)S(1)} %fusion.34, f32[2,5,64,128]{3,2,1,0:T(8,128)S(1)} %fusion.68), channel_id=1, replica_groups=mesh['section'=4,'adapter'=2,'mp'=4] {'mp'}, use_global_device_ids=true, to_apply=%region_1.2 | all-reduce | flops 163840 | bytes 983040 | tf_op jit(solution)/shard_map/psum | solution.py:119
  277.1 8.3 %all_to_all.35 = bf16[2,5,128,2048]{3,2,1,0:T(8,128)(2,1)S(1)} all-to-all(bf16[2,5,128,2048]{3,2,1,0:T(8,128)(2,1)S(1)} %convolution_convert_fusion.4), channel_id=1, replica_groups=mesh['section'=4,'adapter'=2,'mp'=4] {'adapter'}, dimensions={0} | all-to-all | bytes 10485760 | tf_op jit(solution)/shard_map/all_to_all | solution.py:131
  289.9 11.2 %copy.95 = bf16[2,8,128,2048]{3,1,2,0:T(8,128)(2,1)} copy(bf16[2,8,128,2048]{3,2,1,0:T(8,128)(2,1)} %bitcast.142) | data formatting | bytes 16777216
  307.4 8.2 %mul.38 = f32[1024,2048]{1,0:T(8,128)} reshape(f32[8,262144]{1,0:T(8,128)} %convolution_multiply_fusion) | data formatting | bytes 16777216 | tf_op jit(solution)/shard_map/mul | solution.py:162
  321.8 8.1 %all_to_all.36 = bf16[2,5,128,2048]{3,2,1,0:T(8,128)(2,1)S(1)} all-to-all(bf16[2,5,128,2048]{3,2,1,0:T(8,128)(2,1)S(1)} %convolution_convert_fusion.3), channel_id=1, replica_groups=mesh['section'=4,'adapter'=2,'mp'=4] {'adapter'}, dimensions={0} | all-to-all | bytes 10485760 | tf_op jit(solution)/shard_map/all_to_all | solution.py:134
  334.4 11.2 %copy.97 = bf16[2,8,128,2048]{3,1,2,0:T(8,128)(2,1)} copy(bf16[2,8,128,2048]{3,2,1,0:T(8,128)(2,1)} %bitcast.138) | data formatting | bytes 16777216
  351.8 8.1 %reshape.221 = f32[1024,2048]{1,0:T(8,128)} reshape(f32[8,262144]{1,0:T(8,128)} %fusion.48) | data formatting | bytes 16777216 | tf_op jit(solution)/shard_map/reshape | solution.py:94
  359.9 47.7 %all-gather.3.cloned.1.call-done = bf16[1,1024,8192]{2,1,0:T(8,128)(2,1)} async-done(((bf16[1,1024,2048]{2,1,0:T(8,128)(2,1)}), bf16[1,1024,8192]{2,1,0:T(8,128)(2,1)}) %all-gather.3.cloned.1.call-update) | async-done | bytes 16777232 | tf_op jit(solution)/shard_map/all_gather | solution.py:65
  407.6 47.0 %fusion.9 = bf16[1024,2048]{1,0:T(8,128)(2,1)} fusion(f32[1024,2048]{1,0:T(8,128)} %mul.38, bf16[1,1024,2048]{2,1,0:T(8,128)(2,1)} %param.7, bf16[1,8192,2048]{2,1,0:T(8,128)(2,1)} %param.10, bf16[1,1024,8192]{2,1,0:T(8,128)(2,1)} %all-gather.3.cloned.1.call-done), kind=kOutput, calls=%fused_computation.12 | convolution fusion | flops 34368126976 | bytes 67108864 | tf_op jit(solution)/shard_map/dot_general | solution.py:64
  456.0 235.0 %reduce-scatter.2.cloned.1.call-done = bf16[1024,2048]{1,0:T(8,128)(2,1)} async-done(((bf16[1024,8192]{1,0:T(8,128)(2,1)}), bf16[1024,2048]{1,0:T(8,128)(2,1)}) %reduce-scatter.2.cloned.1.call-update) | async-done | bytes 4194320 | tf_op jit(solution)/shard_map/reduce_scatter | solution.py:72
  691.0 8.1 %add_convert_fusion = bf16[1024,2048]{1,0:T(8,128)(2,1)S(1)} fusion(f32[1024,2048]{1,0:T(8,128)} %reshape.221, bf16[1024,2048]{1,0:T(8,128)(2,1)} %reduce-scatter.2.cloned.1.call-done, bf16[1,1024,2048]{2,1,0:T(8,128)(2,1)} %param.9), kind=kLoop, calls=%fused_computation.17 | loop fusion | flops 10485760 | bytes 20971520 | tf_op jit(solution)/shard_map/convert_element_type | solution.py:164
  703.2 9.7 %fusion.28 = bf16[1,8,64,2048]{3,1,2,0:T(8,128)(2,1)S(1)} fusion(f32[2,5,64,2048]{3,2,1,0:T(8,128)S(1)} %convolution_multiply_fusion.1, bf16[2,5,8]{2,1,0:T(8,128)(2,1)S(1)} %all-to-all-done.3), kind=kOutput, calls=%fused_computation.31 | convolution fusion | flops 127926272 | bytes 7340192 | tf_op jit(solution)/shard_map/nkj,nkrm->jrm/dot_general | solution.py:154
  718.7 9.4 %fusion.25 = bf16[1,8,64,2048]{3,1,2,0:T(8,128)(2,1)S(1)} fusion(f32[2,5,64,2048]{3,2,1,0:T(8,128)S(1)} %fusion.47, bf16[2,5,8]{2,1,0:T(8,128)(2,1)S(1)} %all-to-all-done.3), kind=kOutput, calls=%fused_computation.30 | convolution fusion | flops 127926272 | bytes 7340192 | tf_op jit(solution)/shard_map/nkj,nkrm->jrm/dot_general | solution.py:150
  730.6 61.9 %collective-permute-done.1 = bf16[1024,2048]{1,0:T(8,128)(2,1)S(1)} collective-permute-done((bf16[1024,2048]{1,0:T(8,128)(2,1)S(1)}, bf16[1024,2048]{1,0:T(8,128)(2,1)S(1)}, u32[]{:S(2)}, u32[]{:S(2)}) %collective-permute-start.1) | collective-permute-done | bytes 4194336 | tf_op jit(solution)/shard_map/ppermute | solution.py:12
  (63 shorter events, 132.5 us)
Async XLA Ops:
  9.8 34.0 %all-to-all-start.3 = ((bf16[2,5,8]{2,1,0:T(8,128)(2,1)}), bf16[2,5,8]{2,1,0:T(8,128)(2,1)S(1)}, u32[]{:S(2)}, u32[]{:S(2)}) async-start(bf16[2,5,8]{2,1,0:T(8,128)(2,1)} %copy.70), calls=%async_computation.4 | async-start | bytes 8192 | tf_op jit(solution)/shard_map/all_to_all | solution.py:105
  43.8 6.4 copy-start.2
  43.8 11.4 %all-to-all-start.4 = ((bf16[2,5,128,2048]{3,2,1,0:T(8,128)(2,1)}), bf16[2,5,128,2048]{3,2,1,0:T(8,128)(2,1)}, u32[]{:S(2)}, u32[]{:S(2)}) async-start(bf16[2,5,128,2048]{3,2,1,0:T(8,128)(2,1)} %bitcast.147), calls=%async_computation.5 | async-start | bytes 10485760 | tf_op jit(solution)/shard_map/all_to_all | solution.py:101
  49.9 265.6 %all-reduce.4.cloned.1.call-start = ((), (), s32[]{:S(2)}) async-start(), calls=%async_computation.9 | async-start | bytes 655360 | tf_op jit(solution)/shard_map/psum | solution.py:119
  62.7 344.9 %all-gather.3.cloned.1.call-start = ((), (), s32[]{:S(2)}) async-start(), calls=%async_computation.10 | async-start | bytes 20971520 | tf_op jit(solution)/shard_map/all_gather | solution.py:65
  63.5 627.5 %reduce-scatter.2.cloned.1.call-start = ((), (), s32[]{:S(2)}) async-start(), calls=%async_computation.8 | async-start | bytes 20971520 | tf_op jit(solution)/shard_map/reduce_scatter | solution.py:72
  138.1 16.9 %all-to-all-start.6 = ((bf16[2,5,128,2048]{3,2,1,0:T(8,128)(2,1)}), bf16[2,5,128,2048]{3,2,1,0:T(8,128)(2,1)}, u32[]{:S(2)}, u32[]{:S(2)}) async-start(bf16[2,5,128,2048]{3,2,1,0:T(8,128)(2,1)} %bitcast.146), calls=%async_computation.7 | async-start | bytes 10485760 | tf_op jit(solution)/shard_map/all_to_all | solution.py:100
  144.0 7.2 copy-start.1
  155.0 32.8 %all-to-all-start = ((bf16[2,5,8]{1,2,0:T(8,128)(2,1)}), bf16[2,5,8]{1,2,0:T(8,128)(2,1)S(1)}, u32[]{:S(2)}, u32[]{:S(2)}) async-start(bf16[2,5,8]{1,2,0:T(8,128)(2,1)} %copy.63), calls=%async_computation | async-start | bytes 8192 | tf_op jit(solution)/shard_map/all_to_all | solution.py:104
  158.4 6.9 copy-start
  187.8 11.5 %all-to-all-start.1 = ((bf16[2,5,128,2048]{3,2,1,0:T(8,128)(2,1)}), bf16[2,5,128,2048]{3,2,1,0:T(8,128)(2,1)}, u32[]{:S(2)}, u32[]{:S(2)}) async-start(bf16[2,5,128,2048]{3,2,1,0:T(8,128)(2,1)} %bitcast.148), calls=%async_computation.1 | async-start | bytes 10485760 | tf_op jit(solution)/shard_map/all_to_all | solution.py:99
  197.1 74.3 %copy-start.3 = (bf16[1,8,64,2048]{3,2,1,0:T(8,128)(2,1)S(1)}, bf16[1,8,64,2048]{3,2,1,0:T(8,128)(2,1)}, u32[]{:S(2)}) copy-start(bf16[1,8,64,2048]{3,2,1,0:T(8,128)(2,1)} %param.12) | copy-start | bytes 6291460
  454.5 276.1 %collective-permute-start = (bf16[1024,2048]{1,0:T(8,128)(2,1)}, bf16[1024,2048]{1,0:T(8,128)(2,1)}, u32[]{:S(2)}, u32[]{:S(2)}) collective-permute-start(bf16[1024,2048]{1,0:T(8,128)(2,1)} %fusion.9), channel_id=1, source_target_pairs={{0,8},{8,16},{16,24},{24,0},{1,9},{9,17},{17,25},{25,1},{2,10},{10... | collective-permute-start | bytes 12582920 | tf_op jit(solution)/shard_map/ppermute | solution.py:12
  699.2 93.3 %collective-permute-start.1 = (bf16[1024,2048]{1,0:T(8,128)(2,1)S(1)}, bf16[1024,2048]{1,0:T(8,128)(2,1)S(1)}, u32[]{:S(2)}, u32[]{:S(2)}) collective-permute-start(bf16[1024,2048]{1,0:T(8,128)(2,1)S(1)} %add_convert_fusion), channel_id=1, source_target_pairs={{0,24},{8,0},{16,8},{24,16},{1,25},{9,1},{17,9},{25,17},{2,26},{10... | collective-permute-start | bytes 12582920 | tf_op jit(solution)/shard_map/ppermute | solution.py:12
  703.2 12.2 %copy-start.4 = (f32[2,5,64,128]{3,2,1,0:T(8,128)S(1)}, f32[2,5,64,128]{3,2,1,0:T(8,128)}, u32[]{:S(2)}) copy-start(f32[2,5,64,128]{3,2,1,0:T(8,128)} %all-reduce.4.cloned.1.call-done) | copy-start | bytes 983044
Sparse Core Ops, SparseCore 0:
  62.8 36.9 all-reduce.3
  101.4 306.1 all-gather.2
  409.9 281.0 reduce-scatter.1
where the time goes:
time: 815 us; the launch traced here: 806 us
  waiting for transfers between devices  349 us (43%)
  matrix products  194 us (24%)
  local copies, waits for them, and re-layouts  131 us (16%)
  blocking collectives  81.8 us (10%)
  starting transfers between devices  27.2 us (3%)
  between operations  14.4 us (2%)
  other arithmetic  9.73 us (1%)
    reduce_scatter x1, waiting for transfers between devices, local(): lax.psum_scatter(back_term.astype(jnp.bfloat16), 'mp', scatter_dimension=...  235 us
    unnamed x24, local copies, waits for them, and re-layouts  94.2 us
    psum x1, blocking collectives, local(): lax.psum((rank_fwd, rank_back, rank_space_gradient), 'mp')  65.3 us
    ppermute x2, waiting for transfers between devices, shifted(): return lax.ppermute(value, axis, pairs)  61.9 us
    all_gather x1, waiting for transfers between devices, local(): lax.all_gather(hidden_state, 'mp', axis=1, tiled=True)  47.7 us
    dot_general x1, matrix products, local(): jnp.dot(lax.all_gather(hidden_state, 'mp', axis=1, tiled=True), weight, p...  47 us
    dot_general x1, matrix products, local(): lax.dot_general(cotangent, weight, (((1,), (1,)), ((), ())), preferred_el...  42.4 us
    dot_general x3, matrix products, to_slots(): jnp.dot(placing, flat_rows, preferred_element_type=single_float)  22.1 us
  transfers between devices with their start and end apart: 10, of which 5 were waited for; matrix products, arithmetic and copies ran while one was open for 39% of the time, Pallas kernels for 0%

commit v1 on v0

v1 whole, which is shorter than its diff:
```python
import jax
import jax.numpy as jnp
from jax import lax
from jax.sharding import PartitionSpec as P

adapter_scale = 2.0
chunk_count = 2
longest_line = 4


def shifted(value, axis, steps):
    count = lax.axis_size(axis)
    pairs = [(source, (source + steps) % count) for source in range(count)]
    return lax.ppermute(value, axis, pairs)


def line_gather(block, axis):
    n = lax.axis_size(axis)
    me = lax.axis_index(axis)
    up, down = [block], [block]
    for t in range(1, n):
        up.append(lax.ppermute(up[-1], axis, [(j, j + 1) for j in range(t - 1, n - 1)]))
        down.append(lax.ppermute(down[-1], axis, [(j, j - 1) for j in range(1, n - t + 1)]))
    return [block] + [jnp.where(me + k < n, down[k], up[n - k]) for k in range(1, n)]


def line_scatter(terms, axis):
    n = lax.axis_size(axis)
    up = down = None
    for t in range(1, n):
        first, second = terms[n - t], terms[t]
        if up is not None:
            first = (first.astype(jnp.float32) + up.astype(jnp.float32)).astype(jnp.bfloat16)
            second = (second.astype(jnp.float32) + down.astype(jnp.float32)).astype(jnp.bfloat16)
        up = lax.ppermute(first, axis, [(j, j + 1) for j in range(t)])
        down = lax.ppermute(second, axis, [(j, j - 1) for j in range(n - t, n)])
    return terms[0].astype(jnp.float32) + up.astype(jnp.float32) + down.astype(jnp.float32)


def summed(value, axis):
    n = lax.axis_size(axis)
    if n > longest_line or n & (n - 1):
        return lax.psum(value, axis)
    step = 1
    while step < n:
        pairs = [(j, j ^ step) for j in range(n)]
        other = lax.ppermute(value.astype(jnp.bfloat16), axis, pairs)
        value = value + other.astype(jnp.float32)
        step *= 2
    return value


def dot(a, b, a_dim=1, b_dim=0):
    return lax.dot_general(
        a, b, (((a_dim,), (b_dim,)), ((), ())), preferred_element_type=jnp.float32
    )


def local(
    forward_input,
    stored_input,
    output_gradient,
    frozen_weight,
    adapter_down_factor,
    adapter_up_factor,
    adapter_index_list,
):
    f32, bf16 = jnp.float32, jnp.bfloat16
    h, x, g = forward_input[0], stored_input[0], output_gradient[0]
    weight = frozen_weight[0]
    n = lax.axis_size("mp")
    me = lax.axis_index("mp")
    owners = lax.axis_size("adapter")
    core = lax.axis_index("adapter")
    held, rank, width = adapter_down_factor.shape[1:]
    rows = h.shape[0]
    seq_count = adapter_index_list.shape[2]
    seq_len = rows // seq_count
    part = rows // chunk_count
    line = n <= longest_line

    def pieces(value):
        return [value[c * part : (c + 1) * part] for c in range(chunk_count)]

    h_parts, g_parts = pieces(h), pieces(g)

    if line:
        w_blocks = [
            lax.dynamic_slice_in_dim(weight, ((me + k) % n) * width, width, 0) for k in range(n)
        ]
        gathered = [line_gather(piece, "mp") for piece in h_parts]
        back_sums = []
        for piece in g_parts:
            terms = [None] * n
            order = [k for t in range(1, n) for k in (n - t, t)] + [0]
            for k in order:
                if terms[k] is None:
                    terms[k] = dot(piece, w_blocks[k], 1, 1).astype(bf16)
            back_sums.append(line_scatter(terms, "mp"))
        bases = []
        for blocks in gathered:
            base = dot(blocks[0], w_blocks[0])
            for k in range(1, n):
                base = base + dot(blocks[k], w_blocks[k])
            bases.append(base)
    else:
        bases = [
            dot(lax.all_gather(piece, "mp", axis=1, tiled=True), weight) for piece in h_parts
        ]
        back_sums = [
            lax.psum_scatter(
                dot(piece, weight, 1, 1).astype(bf16), "mp", scatter_dimension=1, tiled=True
            ).astype(f32)
            for piece in g_parts
        ]

    def all_tables(table):
        flat = table.reshape(held * rank, width)
        return jnp.concatenate(
            [flat] + [shifted(flat, "adapter", -k) for k in range(1, owners)], axis=0
        )

    down_all = all_tables(adapter_down_factor[0])
    up_all = all_tables(adapter_up_factor[0])
    total = owners * held
    columns = total * rank

    def mask_of(ids):
        place = (ids - core * held + total) % total
        token_place = jnp.repeat(place, seq_len)
        owner = lax.broadcasted_iota(jnp.int32, (rows, columns), 1) // rank
        return token_place[:, None] == owner

    mask_fwd = mask_of(adapter_index_list[0, 0])
    mask_back = mask_of(adapter_index_list[1, 0])
    fold = (
        lax.broadcasted_iota(jnp.int32, (columns, rank), 0) % rank
        == lax.broadcasted_iota(jnp.int32, (columns, rank), 1)
    ).astype(bf16)

    def rank_product(values, table, mask):
        product = jnp.where(mask, dot(values, table, 1, 1), 0.0).astype(bf16)
        return dot(fold, product, 0, 1)

    def spread(code, mask):
        return jnp.where(mask, dot(code, fold, 0, 1), 0.0).astype(bf16)

    ranked = jnp.concatenate(
        [
            rank_product(h, down_all, mask_fwd),
            rank_product(x, down_all, mask_back),
            rank_product(g, up_all, mask_back),
        ],
        axis=1,
    )
    ranked = summed(ranked, "mp")
    u = spread(ranked[:, :rows].astype(bf16), mask_fwd)
    ub = spread(ranked[:, rows : 2 * rows].astype(bf16), mask_back)
    v = spread((adapter_scale * ranked[:, 2 * rows :]).astype(bf16), mask_back)

    def factor_gradient(code, values, scale):
        own = dot(code[:, : held * rank], values, 0, 0)
        for k in range(1, owners):
            theirs = dot(code[:, k * held * rank : (k + 1) * held * rank], values, 0, 0)
            own = own + shifted(theirs.astype(bf16), "adapter", k).astype(f32)
        return (own * scale).astype(bf16).reshape(held, rank, width)

    grad_a = factor_gradient(v, x, 1.0 / seq_len)
    grad_b = factor_gradient(ub, g, adapter_scale / seq_len)

    fwd_next, back_next = [], []
    for c, (u_part, v_part) in enumerate(zip(pieces(u), pieces(v))):
        lora = dot(u_part, up_all).astype(bf16).astype(f32)
        out = h_parts[c].astype(f32) + bases[c] + adapter_scale * lora
        fwd_next.append(shifted(out.astype(bf16), "section", 1))
        w = dot(v_part, down_all).astype(bf16).astype(f32)
        out = g_parts[c].astype(f32) + back_sums[c] + w
        back_next.append(shifted(out.astype(bf16), "section", -1))
    fwd_next = jnp.concatenate(fwd_next, axis=0)
    back_next = jnp.concatenate(back_next, axis=0)
    return (fwd_next[None], back_next[None], grad_a[None], grad_b[None])


def solution(mesh):
    in_specs = (
        P("section", "adapter", "mp"),
        P("section", "adapter", "mp"),
        P("section", "adapter", "mp"),
        P("section", None, "mp"),
        P("section", "adapter", None, "mp"),
        P("section", "adapter", None, "mp"),
        P(None, "section", "adapter"),
    )
    out_specs = (
        P("section", "adapter", "mp"),
        P("section", "adapter", "mp"),
        P("section", "adapter", None, "mp"),
        P("section", "adapter", None, "mp"),
    )
    return jax.shard_map(local, mesh=mesh, in_specs=in_specs, out_specs=out_specs, check_vma=False)
```

time: 815 us -> 877 us (1.076)
  waiting for transfers between devices: 349 us -> 473 us
  local copies, waits for them, and re-layouts: 131 us -> 37.3 us
  blocking collectives: 81.8 us -> 0 us
  starting transfers between devices: 27.2 us -> 84.2 us
  matrix products: 194 us -> 249 us
  between operations: 14.4 us -> 1.39 us
  other arithmetic: 9.73 us -> 19.6 us
    ppermute x0 -> x26, waiting for transfers between devices: none -> 345 us  [the longest x6 161 us: line_gather(): lax.ppermute(up[-1], axis, [(j, j + 1) for j in range(t - 1, n - 1)])]
    reduce_scatter x1 -> x0, waiting for transfers between devices: 235 us -> none  [local(): lax.psum_scatter(back_term.astype(jnp.bfloat16), 'mp', scatter_dimension=...]
    ppermute x0 -> x26, starting transfers between devices: none -> 77.1 us  [the longest x6 30.7 us: line_gather(): lax.ppermute(down[-1], axis, [(j, j - 1) for j in range(1, n - t + 1)])]
    ppermute x2 -> x8, waiting for transfers between devices: 61.9 us -> 128 us  [shifted(): return lax.ppermute(value, axis, pairs)]
    psum x1 -> x0, blocking collectives: 65.3 us -> none  [local(): lax.psum((rank_fwd, rank_back, rank_space_gradient), 'mp')]
    unnamed x24 -> x60, local copies, waits for them, and re-layouts: 94.2 us -> 30.8 us
    dot_general x22 -> x30, matrix products: 194 us -> 249 us  [dot(): lax.dot_general(a, b, (((a_dim,), (b_dim,)), ((), ())), preferred_element...]
    all_gather x1 -> x0, waiting for transfers between devices: 47.7 us -> none  [local(): lax.all_gather(hidden_state, 'mp', axis=1, tiled=True)]
  transfers between devices with their start and end apart: 10 -> 34, of which waited for: 5 -> 14; matrix products, arithmetic and copies ran while one was open for 39% -> 33% of each run, Pallas kernels for 0% -> 0%
where the time goes in v1:
time: 877 us; the launch traced here: 864 us
  waiting for transfers between devices  473 us (54%)
  matrix products  249 us (28%)
  starting transfers between devices  84.2 us (10%)
  local copies, waits for them, and re-layouts  37.3 us (4%)
  other arithmetic  19.6 us (2%)
    dot_general x30, matrix products, dot(): lax.dot_general(a, b, (((a_dim,), (b_dim,)), ((), ())), preferred_element...  249 us
    ppermute x6, waiting for transfers between devices, line_gather(): lax.ppermute(up[-1], axis, [(j, j + 1) for j in range(t - 1, n - 1)])  161 us
    ppermute x2, waiting for transfers between devices, summed(): other = lax.ppermute(value.astype(jnp.bfloat16), axis, pairs)  135 us
    ppermute x8, waiting for transfers between devices, shifted(): return lax.ppermute(value, axis, pairs)  128 us
    ppermute x6, waiting for transfers between devices, line_scatter(): up = lax.ppermute(first, axis, [(j, j + 1) for j in range(t)])  48.7 us
    unnamed x60, local copies, waits for them, and re-layouts  30.8 us
    ppermute x6, starting transfers between devices, line_gather(): lax.ppermute(down[-1], axis, [(j, j - 1) for j in range(1, n - t + 1)])  30.7 us
    ppermute x6, starting transfers between devices, line_gather(): lax.ppermute(up[-1], axis, [(j, j + 1) for j in range(t - 1, n - 1)])  18.7 us
  transfers between devices with their start and end apart: 34, of which 14 were waited for; matrix products, arithmetic and copies ran while one was open for 33% of the time, Pallas kernels for 0%

profile of v1, /device:TPU:18, one launch (start us, length us, event | category | flops | bytes accessed | tf_op | source)
XLA Modules:
  0.0 864.0 jit_solution(7578646428342759829)
XLA Ops:
  34.7 10.7 %fusion.28 = f32[2048,512]{1,0:T(8,128)} fusion(bf16[1,8192,2048]{2,1,0:T(8,128)(2,1)} %param.10, s32[]{:T(128)S(6)} %select_n.117, bf16[1,1024,2048]{2,1,0:T(8,128)(2,1)} %param.7), kind=kOutput, calls=%fused_computation.28 | convolution fusion | flops 4294967296 | bytes 14680068 | tf_op jit(solution)/shard_map/dot_general | solution.py:54
  45.4 10.0 %fusion.30 = f32[2048,512]{1,0:T(8,128)} fusion(bf16[1,8192,2048]{2,1,0:T(8,128)(2,1)} %param.10, s32[]{:T(128)S(6)} %select_n.117, bf16[1,1024,2048]{2,1,0:T(8,128)(2,1)S(1)} %copy-done.1), kind=kOutput, calls=%fused_computation.30 | convolution fusion | flops 4294967296 | bytes 14680068 | tf_op jit(solution)/shard_map/dot_general | solution.py:54
  85.8 10.1 %fusion.133 = bf16[512,2048]{0,1:T(8,128)(2,1)} fusion(bf16[1,8192,2048]{2,1,0:T(8,128)(2,1)} %param.10, s32[]{:T(128)S(6)} %select_n.129, bf16[1,1024,2048]{2,1,0:T(8,128)(2,1)} %param.9), kind=kOutput, calls=%fused_computation.131 | convolution fusion | flops 4296015872 | bytes 12582916 | tf_op jit(solution)/shard_map/dot_general | solution.py:54
  141.4 12.2 %fusion.60 = (bf16[512,2048]{0,1:T(8,128)(2,1)}, bf16[512,2048]{0,1:T(8,128)(2,1)}) fusion(bf16[512,2048]{0,1:T(8,128)(2,1)} %collective-permute-done.25, bf16[512,2048]{0,1:T(8,128)(2,1)} %collective-permute-done.28, bf16[1,1024,2048]{2,1,0:T(8,128)(2,1)} %param.9, bf16[1,8192,2048]{2,1,0:T(8,128)(2,1)} %param.10, s32[]{:T(128)S(6)} %select_n.125), kind=kOutput, calls=%fused_computation.68 | convolution fusion | flops 4303355904 | bytes 18874372 | tf_op jit(solution)/shard_map/dot_general | solution.py:54
  153.6 41.2 %collective-permute-done.8 = bf16[64,3072]{1,0:T(8,128)(2,1)S(1)} collective-permute-done((bf16[64,3072]{1,0:T(8,128)(2,1)S(1)}, bf16[64,3072]{1,0:T(8,128)(2,1)S(1)}, u32[]{:S(2)}, u32[]{:S(2)}) %collective-permute-start.8) | collective-permute-done | bytes 393248 | tf_op jit(solution)/shard_map/ppermute | solution.py:47
  194.7 16.1 %collective-permute-start = (bf16[512,2048]{0,1:T(8,128)(2,1)S(1)}, bf16[512,2048]{0,1:T(8,128)(2,1)}, u32[]{:S(2)}, u32[]{:S(2)}) collective-permute-start(bf16[512,2048]{0,1:T(8,128)(2,1)S(1)} %bitcast.243), channel_id=1, source_target_pairs={{1,0},{2,1},{3,2},{5,4},{6,5},{7,6},{9,8},{10,9},{11,10},{13,12},{... | collective-permute-start | bytes 6291464 | tf_op jit(solution)/shard_map/ppermute | solution.py:23
  213.0 10.6 %fusion.66 = (bf16[512,2048]{0,1:T(8,128)(2,1)}, bf16[512,2048]{0,1:T(8,128)(2,1)}) fusion(bf16[512,2048]{0,1:T(8,128)(2,1)} %collective-permute-done.18, bf16[512,2048]{0,1:T(8,128)(2,1)} %collective-permute-done.21, bf16[1,1024,2048]{2,1,0:T(8,128)(2,1)S(1)} %copy-done.4, bf16[1,8192,2048]{2,1,0:T(8,128)(2,1)} %param.10, s32[]{:T(128)S(6)} %select_n.125), kind=kOutput, calls=%fused_computation.77 | convolution fusion | flops 4303355904 | bytes 18874372 | tf_op jit(solution)/shard_map/dot_general | solution.py:54
  223.6 93.4 %collective-permute-done.9 = bf16[64,3072]{1,0:T(8,128)(2,1)S(1)} collective-permute-done((bf16[64,3072]{1,0:T(8,128)(2,1)S(1)}, bf16[64,3072]{1,0:T(8,128)(2,1)S(1)}, u32[]{:S(2)}, u32[]{:S(2)}) %collective-permute-start.9) | collective-permute-done | bytes 393248 | tf_op jit(solution)/shard_map/ppermute | solution.py:47
  372.7 40.1 %collective-permute-done.1 = bf16[512,2048]{0,1:T(8,128)(2,1)S(1)} collective-permute-done((bf16[512,2048]{0,1:T(8,128)(2,1)S(1)}, bf16[512,2048]{0,1:T(8,128)(2,1)S(1)}, u32[]{:S(2)}, u32[]{:S(2)}) %collective-permute-start.1) | collective-permute-done | bytes 2097184 | tf_op jit(solution)/shard_map/ppermute | solution.py:22
  419.5 38.3 %collective-permute-done.13 = bf16[512,2048]{0,1:T(8,128)(2,1)S(1)} collective-permute-done((bf16[512,2048]{0,1:T(8,128)(2,1)S(1)}, bf16[512,2048]{0,1:T(8,128)(2,1)S(1)}, u32[]{:S(2)}, u32[]{:S(2)}) %collective-permute-start.13) | collective-permute-done | bytes 2097184 | tf_op jit(solution)/shard_map/ppermute | solution.py:22
  459.1 10.7 %fusion.12 = f32[512,2048]{0,1:T(8,128)} fusion(bf16[1,8192,2048]{2,1,0:T(8,128)(2,1)} %param.10, s32[]{:T(128)S(6)} %select_n.125, bf16[512,2048]{0,1:T(8,128)(2,1)} %copy-done.17, bf16[512,2048]{0,1:T(8,128)(2,1)} %copy-done.19, pred[]{:T(512)S(6)} %lt.73), kind=kOutput, calls=%fused_computation.12 | convolution fusion | flops 4296015872 | bytes 16777220 | tf_op jit(solution)/shard_map/dot_general | solution.py:54
  474.9 27.8 %collective-permute-done.19 = bf16[512,2048]{0,1:T(8,128)(2,1)S(1)} collective-permute-done((bf16[512,2048]{0,1:T(8,128)(2,1)S(1)}, bf16[512,2048]{0,1:T(8,128)(2,1)S(1)}, u32[]{:S(2)}, u32[]{:S(2)}) %collective-permute-start.19) | collective-permute-done | bytes 2097184 | tf_op jit(solution)/shard_map/ppermute | solution.py:35
  507.5 37.5 %collective-permute-done.2 = bf16[512,2048]{0,1:T(8,128)(2,1)} collective-permute-done((bf16[512,2048]{0,1:T(8,128)(2,1)S(1)}, bf16[512,2048]{0,1:T(8,128)(2,1)}, u32[]{:S(2)}, u32[]{:S(2)}) %collective-permute-start.2) | collective-permute-done | bytes 2097184 | tf_op jit(solution)/shard_map/ppermute | solution.py:22
  546.9 10.6 %fusion.14 = f32[512,2048]{0,1:T(8,128)} fusion(bf16[1,8192,2048]{2,1,0:T(8,128)(2,1)} %param.10, s32[]{:T(128)S(6)} %select_n.125, bf16[512,2048]{0,1:T(8,128)(2,1)} %collective-permute-done.4, bf16[512,2048]{0,1:T(8,128)(2,1)} %collective-permute-done.2, pred[]{:T(512)S(6)} %lt.73), kind=kOutput, calls=%fused_computation.14 | convolution fusion | flops 4296015872 | bytes 16777220 | tf_op jit(solution)/shard_map/dot_general | solution.py:54
  560.4 10.6 %fusion.20 = f32[512,2048]{0,1:T(8,128)} fusion(bf16[1,8192,2048]{2,1,0:T(8,128)(2,1)} %param.10, s32[]{:T(128)S(6)} %select_n.121, bf16[512,2048]{0,1:T(8,128)(2,1)} %collective-permute-done.11, bf16[512,2048]{0,1:T(8,128)(2,1)S(1)} %collective-permute-done.14, pred[]{:T(512)S(6)} %lt.70), kind=kOutput, calls=%fused_computation.20 | convolution fusion | flops 4296015872 | bytes 16777220 | tf_op jit(solution)/shard_map/dot_general | solution.py:54
  574.5 15.6 %fusion.76 = bf16[512,2048]{0,1:T(8,128)(2,1)} fusion(f32[512,2048]{0,1:T(8,128)} %fusion.12, f32[512,2048]{0,1:T(8,128)} %fusion.20, f32[2048,512]{1,0:T(8,128)} %fusion.28, bf16[512,2048]{0,1:T(8,128)(2,1)} %convolution_convert_fusion.2, bf16[1,8192,2048]{2,1,0:T(8,128)(2,1)} %param.10, s32[]{:T(128)S(6)} %select_n.129, bf16[512,2048]{0,1:T(8,128)(2,1)} %copy-done.22, ...), kind=kOutput, calls=%fused_computation.89 | convolution fusion | flops 4305453056 | bytes 31457284 | tf_op jit(solution)/shard_map/dot_general | solution.py:54
  590.1 44.8 %collective-permute-done.3 = bf16[512,2048]{0,1:T(8,128)(2,1)} collective-permute-done((bf16[512,2048]{0,1:T(8,128)(2,1)}, bf16[512,2048]{0,1:T(8,128)(2,1)}, u32[]{:S(2)}, u32[]{:S(2)}) %collective-permute-start.3) | collective-permute-done | bytes 2097184 | tf_op jit(solution)/shard_map/ppermute | solution.py:22
  637.2 10.6 %fusion.22 = f32[512,2048]{0,1:T(8,128)} fusion(bf16[1,8192,2048]{2,1,0:T(8,128)(2,1)} %param.10, s32[]{:T(128)S(6)} %select_n.121, bf16[512,2048]{0,1:T(8,128)(2,1)} %collective-permute-done, bf16[512,2048]{0,1:T(8,128)(2,1)} %collective-permute-done.3, pred[]{:T(512)S(6)} %lt.70), kind=kOutput, calls=%fused_computation.22 | convolution fusion | flops 4296015872 | bytes 16777220 | tf_op jit(solution)/shard_map/dot_general | solution.py:54
  653.1 15.6 %fusion.95 = bf16[512,2048]{0,1:T(8,128)(2,1)} fusion(f32[512,2048]{0,1:T(8,128)} %fusion.14, f32[512,2048]{0,1:T(8,128)} %fusion.22, f32[2048,512]{1,0:T(8,128)} %fusion.30, bf16[512,2048]{0,1:T(8,128)(2,1)} %convolution_convert_fusion.3, bf16[1,8192,2048]{2,1,0:T(8,128)(2,1)} %param.10, s32[]{:T(128)S(6)} %select_n.129, ...), kind=kOutput, calls=%fused_computation.109 | convolution fusion | flops 4305453056 | bytes 31457284 | tf_op jit(solution)/shard_map/dot_general | solution.py:54
  670.5 10.2 %fusion.65 = bf16[512,2048]{0,1:T(8,128)(2,1)} fusion(bf16[2048,512]{1,0:T(8,128)(2,1)} %fusion.109, bf16[512,2048]{0,1:T(8,128)(2,1)} %collective-permute-done.30, bf16[512,2048]{0,1:T(8,128)(2,1)} %collective-permute-done.27, bf16[1,512,2048]{1,2,0:T(8,128)(2,1)} %copy.40, bf16[1024,1024]{1,0:T(8,128)(2,1)} %copy-done.23, ...), kind=kOutput, calls=%fused_computation.74 | convolution fusion | flops 2167406592 | bytes 15728640 | tf_op jit(solution)/shard_map/dot_general | solution.py:54
  682.8 12.2 %collective-permute-done.20 = bf16[512,2048]{0,1:T(8,128)(2,1)} collective-permute-done((bf16[512,2048]{0,1:T(8,128)(2,1)}, bf16[512,2048]{0,1:T(8,128)(2,1)}, u32[]{:S(2)}, u32[]{:S(2)}) %collective-permute-start.20) | collective-permute-done | bytes 2097184 | tf_op jit(solution)/shard_map/ppermute | solution.py:35
  717.7 44.9 %collective-permute-done.10 = bf16[512,2048]{0,1:T(8,128)(2,1)S(1)} collective-permute-done((bf16[512,2048]{0,1:T(8,128)(2,1)S(1)}, bf16[512,2048]{0,1:T(8,128)(2,1)S(1)}, u32[]{:S(2)}, u32[]{:S(2)}) %collective-permute-start.10) | collective-permute-done | bytes 2097184 | tf_op jit(solution)/shard_map/ppermute | solution.py:14
  771.6 36.9 %collective-permute-done.31 = bf16[512,2048]{0,1:T(8,128)(2,1)S(1)} collective-permute-done((bf16[512,2048]{0,1:T(8,128)(2,1)}, bf16[512,2048]{0,1:T(8,128)(2,1)S(1)}, u32[]{:S(2)}, u32[]{:S(2)}) %collective-permute-start.31) | collective-permute-done | bytes 2097184 | tf_op jit(solution)/shard_map/ppermute | solution.py:14
  808.5 44.6 %collective-permute-done.24 = bf16[512,2048]{0,1:T(8,128)(2,1)} collective-permute-done((bf16[512,2048]{0,1:T(8,128)(2,1)}, bf16[512,2048]{0,1:T(8,128)(2,1)}, u32[]{:S(2)}, u32[]{:S(2)}) %collective-permute-start.24) | collective-permute-done | bytes 2097184 | tf_op jit(solution)/shard_map/ppermute | solution.py:14
  (151 shorter events, 247.3 us)
Async XLA Ops:
  8.5 322.2 %collective-permute-start.11 = (bf16[512,2048]{0,1:T(8,128)(2,1)}, bf16[512,2048]{0,1:T(8,128)(2,1)}, u32[]{:S(2)}, u32[]{:S(2)}) collective-permute-start(bf16[512,2048]{0,1:T(8,128)(2,1)} %bitcast.241), channel_id=1, source_target_pairs={{1,0},{2,1},{3,2},{5,4},{6,5},{7,6},{9,8},{10,9},{11,10},{13,12},{... | collective-permute-start | bytes 6291464 | tf_op jit(solution)/shard_map/ppermute | solution.py:23
  10.9 93.2 %collective-permute-start.7 = (bf16[512,2048]{1,0:T(8,128)(2,1)}, bf16[512,2048]{1,0:T(8,128)(2,1)}, u32[]{:S(2)}, u32[]{:S(2)}) collective-permute-start(bf16[512,2048]{1,0:T(8,128)(2,1)} %bitcast.245), channel_id=1, source_target_pairs={{0,4},{4,0},{1,5},{5,1},{2,6},{6,2},{3,7},{7,3},{8,12},{12,8},{9,1... | collective-permute-start | bytes 6291464 | tf_op jit(solution)/shard_map/ppermute | solution.py:14
  11.0 103.7 %collective-permute-start.6 = (bf16[512,2048]{1,0:T(8,128)(2,1)}, bf16[512,2048]{1,0:T(8,128)(2,1)}, u32[]{:S(2)}, u32[]{:S(2)}) collective-permute-start(bf16[512,2048]{1,0:T(8,128)(2,1)} %bitcast.249), channel_id=1, source_target_pairs={{0,4},{4,0},{1,5},{5,1},{2,6},{6,2},{3,7},{7,3},{8,12},{12,8},{9,1... | collective-permute-start | bytes 6291464 | tf_op jit(solution)/shard_map/ppermute | solution.py:14
  21.3 112.0 %collective-permute-start.25 = (bf16[512,2048]{0,1:T(8,128)(2,1)}, bf16[512,2048]{0,1:T(8,128)(2,1)}, u32[]{:S(2)}, u32[]{:S(2)}) collective-permute-start(bf16[512,2048]{0,1:T(8,128)(2,1)} %fusion.130), channel_id=1, source_target_pairs={{0,1},{4,5},{8,9},{12,13},{16,17},{20,21},{24,25},{28,29}} | collective-permute-start | bytes 6291464 | tf_op jit(solution)/shard_map/ppermute | solution.py:35
  33.2 108.1 %collective-permute-start.28 = (bf16[512,2048]{0,1:T(8,128)(2,1)}, bf16[512,2048]{0,1:T(8,128)(2,1)}, u32[]{:S(2)}, u32[]{:S(2)}) collective-permute-start(bf16[512,2048]{0,1:T(8,128)(2,1)} %fusion.136), channel_id=1, source_target_pairs={{3,2},{7,6},{11,10},{15,14},{19,18},{23,22},{27,26},{31,30}} | collective-permute-start | bytes 6291464 | tf_op jit(solution)/shard_map/ppermute | solution.py:36
  104.1 106.8 %collective-permute-start.18 = (bf16[512,2048]{0,1:T(8,128)(2,1)}, bf16[512,2048]{0,1:T(8,128)(2,1)}, u32[]{:S(2)}, u32[]{:S(2)}) collective-permute-start(bf16[512,2048]{0,1:T(8,128)(2,1)} %fusion.133), channel_id=1, source_target_pairs={{0,1},{4,5},{8,9},{12,13},{16,17},{20,21},{24,25},{28,29}} | collective-permute-start | bytes 6291464 | tf_op jit(solution)/shard_map/ppermute | solution.py:35
  114.7 98.2 %collective-permute-start.21 = (bf16[512,2048]{0,1:T(8,128)(2,1)S(1)}, bf16[512,2048]{0,1:T(8,128)(2,1)}, u32[]{:S(2)}, u32[]{:S(2)}) collective-permute-start(bf16[512,2048]{0,1:T(8,128)(2,1)S(1)} %fusion.139), channel_id=1, source_target_pairs={{3,2},{7,6},{11,10},{15,14},{19,18},{23,22},{27,26},{31,30}} | collective-permute-start | bytes 6291464 | tf_op jit(solution)/shard_map/ppermute | solution.py:36
  133.3 199.4 %collective-permute-start.12 = (bf16[512,2048]{0,1:T(8,128)(2,1)}, bf16[512,2048]{0,1:T(8,128)(2,1)S(1)}, u32[]{:S(2)}, u32[]{:S(2)}) collective-permute-start(bf16[512,2048]{0,1:T(8,128)(2,1)} %bitcast.242), channel_id=1, source_target_pairs={{0,1},{1,2},{2,3},{4,5},{5,6},{6,7},{8,9},{9,10},{10,11},{12,13},{... | collective-permute-start | bytes 6291464 | tf_op jit(solution)/shard_map/ppermute | solution.py:22
  194.7 142.7 %collective-permute-start = (bf16[512,2048]{0,1:T(8,128)(2,1)S(1)}, bf16[512,2048]{0,1:T(8,128)(2,1)}, u32[]{:S(2)}, u32[]{:S(2)}) collective-permute-start(bf16[512,2048]{0,1:T(8,128)(2,1)S(1)} %bitcast.243), channel_id=1, source_target_pairs={{1,0},{2,1},{3,2},{5,4},{6,5},{7,6},{9,8},{10,9},{11,10},{13,12},{... | collective-permute-start | bytes 6291464 | tf_op jit(solution)/shard_map/ppermute | solution.py:23
  211.0 140.5 %collective-permute-start.29 = (bf16[512,2048]{0,1:T(8,128)(2,1)}, bf16[512,2048]{0,1:T(8,128)(2,1)S(1)}, u32[]{:S(2)}, u32[]{:S(2)}) collective-permute-start(bf16[512,2048]{0,1:T(8,128)(2,1)} %get-tuple-element.17), channel_id=1, source_target_pairs={{2,1},{3,2},{6,5},{7,6},{10,9},{11,10},{14,13},{15,14},{18,17},{19... | collective-permute-start | bytes 6291464 | tf_op jit(solution)/shard_map/ppermute | solution.py:36
  212.9 104.0 %collective-permute-start.9 = (bf16[64,3072]{1,0:T(8,128)(2,1)S(1)}, bf16[64,3072]{1,0:T(8,128)(2,1)S(1)}, u32[]{:S(2)}, u32[]{:S(2)}) collective-permute-start(bf16[64,3072]{1,0:T(8,128)(2,1)S(1)} %fusion.200), channel_id=1, source_target_pairs={{0,2},{1,3},{2,0},{3,1},{4,6},{5,7},{6,4},{7,5},{8,10},{9,11},{10,... | collective-permute-start | bytes 1179656 | tf_op jit(solution)/shard_map/ppermute | solution.py:47
  330.8 82.0 %collective-permute-start.1 = (bf16[512,2048]{0,1:T(8,128)(2,1)S(1)}, bf16[512,2048]{0,1:T(8,128)(2,1)S(1)}, u32[]{:S(2)}, u32[]{:S(2)}) collective-permute-start(bf16[512,2048]{0,1:T(8,128)(2,1)S(1)} %bitcast.244), channel_id=1, source_target_pairs={{0,1},{1,2},{2,3},{4,5},{5,6},{6,7},{8,9},{9,10},{10,11},{12,13},{... | collective-permute-start | bytes 6291464 | tf_op jit(solution)/shard_map/ppermute | solution.py:22
  332.7 84.7 %collective-permute-start.15 = (bf16[512,2048]{0,1:T(8,128)(2,1)}, bf16[512,2048]{0,1:T(8,128)(2,1)S(1)}, u32[]{:S(2)}, u32[]{:S(2)}) collective-permute-start(bf16[512,2048]{0,1:T(8,128)(2,1)} %collective-permute-done.11), channel_id=1, source_target_pairs={{1,0},{2,1},{5,4},{6,5},{9,8},{10,9},{13,12},{14,13},{17,16},{18,1... | collective-permute-start | bytes 6291464 | tf_op jit(solution)/shard_map/ppermute | solution.py:23
  337.4 120.3 %collective-permute-start.13 = (bf16[512,2048]{0,1:T(8,128)(2,1)S(1)}, bf16[512,2048]{0,1:T(8,128)(2,1)S(1)}, u32[]{:S(2)}, u32[]{:S(2)}) collective-permute-start(bf16[512,2048]{0,1:T(8,128)(2,1)S(1)} %collective-permute-done.12), channel_id=1, source_target_pairs={{1,2},{2,3},{5,6},{6,7},{9,10},{10,11},{13,14},{14,15},{17,18},{18... | collective-permute-start | bytes 6291464 | tf_op jit(solution)/shard_map/ppermute | solution.py:22
  351.5 118.3 %collective-permute-start.22 = (bf16[512,2048]{0,1:T(8,128)(2,1)}, bf16[512,2048]{0,1:T(8,128)(2,1)S(1)}, u32[]{:S(2)}, u32[]{:S(2)}) collective-permute-start(bf16[512,2048]{0,1:T(8,128)(2,1)} %get-tuple-element.15), channel_id=1, source_target_pairs={{2,1},{3,2},{6,5},{7,6},{10,9},{11,10},{14,13},{15,14},{18,17},{19... | collective-permute-start | bytes 6291464 | tf_op jit(solution)/shard_map/ppermute | solution.py:36
  367.9 134.8 %collective-permute-start.19 = (bf16[512,2048]{0,1:T(8,128)(2,1)S(1)}, bf16[512,2048]{0,1:T(8,128)(2,1)S(1)}, u32[]{:S(2)}, u32[]{:S(2)}) collective-permute-start(bf16[512,2048]{0,1:T(8,128)(2,1)S(1)} %copy-done.16), channel_id=1, source_target_pairs={{0,1},{1,2},{4,5},{5,6},{8,9},{9,10},{12,13},{13,14},{16,17},{17,1... | collective-permute-start | bytes 6291464 | tf_op jit(solution)/shard_map/ppermute | solution.py:35
  412.8 92.6 %collective-permute-start.4 = (bf16[512,2048]{0,1:T(8,128)(2,1)}, bf16[512,2048]{0,1:T(8,128)(2,1)}, u32[]{:S(2)}, u32[]{:S(2)}) collective-permute-start(bf16[512,2048]{0,1:T(8,128)(2,1)} %collective-permute-done), channel_id=1, source_target_pairs={{1,0},{2,1},{5,4},{6,5},{9,8},{10,9},{13,12},{14,13},{17,16},{18,1... | collective-permute-start | bytes 6291464 | tf_op jit(solution)/shard_map/ppermute | solution.py:23
  417.4 127.7 %collective-permute-start.2 = (bf16[512,2048]{0,1:T(8,128)(2,1)S(1)}, bf16[512,2048]{0,1:T(8,128)(2,1)}, u32[]{:S(2)}, u32[]{:S(2)}) collective-permute-start(bf16[512,2048]{0,1:T(8,128)(2,1)S(1)} %collective-permute-done.1), channel_id=1, source_target_pairs={{1,2},{2,3},{5,6},{6,7},{9,10},{10,11},{13,14},{14,15},{17,18},{18... | collective-permute-start | bytes 6291464 | tf_op jit(solution)/shard_map/ppermute | solution.py:22
  459.1 244.3 %collective-permute-start.32 = (bf16[512,2048]{1,0:T(8,128)(2,1)}, bf16[512,2048]{1,0:T(8,128)(2,1)}, u32[]{:S(2)}, u32[]{:S(2)}) collective-permute-start(bf16[512,2048]{1,0:T(8,128)(2,1)} %fusion.100), channel_id=1, source_target_pairs={{0,4},{4,0},{1,5},{5,1},{2,6},{6,2},{3,7},{7,3},{8,12},{12,8},{9,1... | collective-permute-start | bytes 6291464 | tf_op jit(solution)/shard_map/ppermute | solution.py:14
  469.8 87.7 %collective-permute-start.14 = (bf16[512,2048]{0,1:T(8,128)(2,1)S(1)}, bf16[512,2048]{0,1:T(8,128)(2,1)S(1)}, u32[]{:S(2)}, u32[]{:S(2)}) collective-permute-start(bf16[512,2048]{0,1:T(8,128)(2,1)S(1)} %copy-done.20), channel_id=1, source_target_pairs={{2,3},{6,7},{10,11},{14,15},{18,19},{22,23},{26,27},{30,31}} | collective-permute-start | bytes 6291464 | tf_op jit(solution)/shard_map/ppermute | solution.py:22
  505.4 163.3 %collective-permute-start.30 = (bf16[512,2048]{0,1:T(8,128)(2,1)}, bf16[512,2048]{0,1:T(8,128)(2,1)}, u32[]{:S(2)}, u32[]{:S(2)}) collective-permute-start(bf16[512,2048]{0,1:T(8,128)(2,1)} %add_convert_fusion), channel_id=1, source_target_pairs={{1,0},{2,1},{3,2},{5,4},{6,5},{7,6},{9,8},{10,9},{11,10},{13,12},{... | collective-permute-start | bytes 6291464 | tf_op jit(solution)/shard_map/ppermute | solution.py:36
  545.0 123.8 %collective-permute-start.27 = (bf16[512,2048]{0,1:T(8,128)(2,1)}, bf16[512,2048]{0,1:T(8,128)(2,1)}, u32[]{:S(2)}, u32[]{:S(2)}) collective-permute-start(bf16[512,2048]{0,1:T(8,128)(2,1)} %add_convert_fusion.1), channel_id=1, source_target_pairs={{0,1},{1,2},{2,3},{4,5},{5,6},{6,7},{8,9},{9,10},{10,11},{12,13},{... | collective-permute-start | bytes 6291464 | tf_op jit(solution)/shard_map/ppermute | solution.py:35
  695.0 113.5 %collective-permute-start.31 = (bf16[512,2048]{0,1:T(8,128)(2,1)}, bf16[512,2048]{0,1:T(8,128)(2,1)S(1)}, u32[]{:S(2)}, u32[]{:S(2)}) collective-permute-start(bf16[512,2048]{0,1:T(8,128)(2,1)} %fusion.65), channel_id=1, source_target_pairs={{0,24},{8,0},{16,8},{24,16},{1,25},{9,1},{17,9},{25,17},{2,26},{10... | collective-permute-start | bytes 6291464 | tf_op jit(solution)/shard_map/ppermute | solution.py:14
  703.3 149.7 %collective-permute-start.24 = (bf16[512,2048]{0,1:T(8,128)(2,1)}, bf16[512,2048]{0,1:T(8,128)(2,1)}, u32[]{:S(2)}, u32[]{:S(2)}) collective-permute-start(bf16[512,2048]{0,1:T(8,128)(2,1)} %fusion.71), channel_id=1, source_target_pairs={{0,24},{8,0},{16,8},{24,16},{1,25},{9,1},{17,9},{25,17},{2,26},{10... | collective-permute-start | bytes 6291464 | tf_op jit(solution)/shard_map/ppermute | solution.py:14
  (37 other events, 1159.0 us)

commit v2 on v1

v2 whole, which is shorter than its diff:
```python
import functools

import jax
import jax.numpy as jnp
from jax import lax
from jax.experimental import pallas as pl
from jax.experimental.pallas import tpu as pltpu
from jax.sharding import PartitionSpec as P

adapter_scale = 2.0
chunk_count = 4
longest_line = 4


def shifted(value, axis, steps):
    count = lax.axis_size(axis)
    pairs = [(source, (source + steps) % count) for source in range(count)]
    return lax.ppermute(value, axis, pairs)


def relay_kernel(
    n, chunks, h, g, weight, fwd_add, back_add,
    fwd_next, back_next, blocks, arrived, sending, results,
    gather_send, gather_recv, sum_send, sum_recv, relay_send, relay_recv, own_sem,
):
    me = lax.axis_index("mp")
    section = lax.axis_index("section")
    sections = lax.axis_size("section")
    after = lax.rem(section + 1, sections)
    before = lax.rem(section + sections - 1, sections)
    rows, width = h.shape
    part = rows // chunks
    tile = min(512, width)
    narrow = min(256, width)
    mesh_id = pl.DeviceIdType.MESH

    def here(c):
        return pl.ds(pl.multiple_of(c * part, part), part)

    barrier = pltpu.get_barrier_semaphore()
    for other in (after, before):
        pl.semaphore_signal(barrier, 1, device_id={"section": other}, device_id_type=mesh_id)

    @pl.when(me > 0)
    def _():
        pl.semaphore_signal(barrier, 1, device_id={"mp": me - 1}, device_id_type=mesh_id)

    @pl.when(me < n - 1)
    def _():
        pl.semaphore_signal(barrier, 1, device_id={"mp": me + 1}, device_id_type=mesh_id)

    pl.semaphore_wait(barrier, 2 + (me > 0).astype(jnp.int32) + (me < n - 1).astype(jnp.int32))

    own = pltpu.make_async_copy(h, blocks.at[me], own_sem)
    own.start()

    def position(way):
        return me + way * (n - 1 - 2 * me)

    def toward(way):
        return me + 1 - 2 * way

    def gather_copy(way, t, c):
        block = me - (1 - 2 * way) * (t - 1)
        return pltpu.make_async_remote_copy(
            src_ref=h.at[here(c)] if isinstance(t, int) and t == 1 else blocks.at[block, here(c)],
            dst_ref=blocks.at[block, here(c)],
            send_sem=gather_send.at[way, t, c],
            recv_sem=gather_recv.at[way, t, c],
            device_id={"mp": toward(way)},
            device_id_type=mesh_id,
        )

    def gather_wait(way, t, c):
        block = me - (1 - 2 * way) * t
        pltpu.make_async_copy(
            blocks.at[block, here(c)], blocks.at[block, here(c)], gather_recv.at[way, t, c]
        ).wait()

    def sum_copy(way, t, c):
        block = me + (1 - 2 * way) * (n - t)
        return pltpu.make_async_remote_copy(
            src_ref=sending.at[block, here(c)],
            dst_ref=arrived.at[way, t, here(c)],
            send_sem=sum_send.at[way, t, c],
            recv_sem=sum_recv.at[way, t, c],
            device_id={"mp": toward(way)},
            device_id_type=mesh_id,
        )

    def sum_wait(way, t, c):
        pltpu.make_async_copy(
            arrived.at[way, t, here(c)], arrived.at[way, t, here(c)], sum_recv.at[way, t, c]
        ).wait()

    def relay_copy(which, c):
        return pltpu.make_async_remote_copy(
            src_ref=results.at[which, here(c)],
            dst_ref=(fwd_next, back_next)[which].at[here(c)],
            send_sem=relay_send.at[which, c],
            recv_sem=relay_recv.at[which, c],
            device_id={"section": (after, before)[which]},
            device_id_type=mesh_id,
        )

    def weight_rows(block):
        return weight.at[pl.ds(pl.multiple_of(block * width, width), width)]

    def product(block, c):
        return (
            [
                pl.BlockSpec((part, width), lambda j: (0, 0)),
                pl.BlockSpec((tile, width), lambda j: (j, 0)),
            ],
            [g.at[here(c)], weight_rows(block)],
        )

    piece = pl.BlockSpec((part, tile), lambda j: (0, j))

    def first_sum(block, c):
        def body(g_ref, w_ref, out_ref):
            out_ref[...] = dot(g_ref[...], w_ref[...], 1, 1).astype(jnp.bfloat16)

        specs, refs = product(block, c)
        pltpu.emit_pipeline(
            body, grid=(width // tile,), in_specs=specs, out_specs=[piece]
        )(*refs, sending.at[block, here(c)])

    def later_sum(way, t, block, c):
        def body(g_ref, w_ref, old_ref, out_ref):
            term = dot(g_ref[...], w_ref[...], 1, 1)
            out_ref[...] = (term + old_ref[...].astype(jnp.float32)).astype(jnp.bfloat16)

        specs, refs = product(block, c)
        pltpu.emit_pipeline(
            body, grid=(width // tile,), in_specs=specs + [piece], out_specs=[piece]
        )(*refs, arrived.at[way, t - 1, here(c)], sending.at[block, here(c)])

    def last_sum(c):
        def body(g_ref, w_ref, up_ref, down_ref, add_ref, out_ref):
            total = dot(g_ref[...], w_ref[...], 1, 1) + add_ref[...]
            up = jnp.where(me > 0, up_ref[...].astype(jnp.float32), 0.0)
            down = jnp.where(me < n - 1, down_ref[...].astype(jnp.float32), 0.0)
            out_ref[...] = (total + up + down).astype(jnp.bfloat16)

        specs, refs = product(me, c)
        pltpu.emit_pipeline(
            body, grid=(width // tile,), in_specs=specs + [piece] * 3, out_specs=[piece]
        )(
            *refs,
            arrived.at[0, n - 1, here(c)],
            arrived.at[1, n - 1, here(c)],
            back_add.at[here(c)],
            results.at[1, here(c)],
        )

    def base(c):
        def body(b_ref, w_ref, add_ref, out_ref):
            total = add_ref[...]
            for k in range(n):
                total = total + dot(b_ref[k], w_ref[k * width : (k + 1) * width, :])
            out_ref[...] = total.astype(jnp.bfloat16)

        strip = pl.BlockSpec((part, narrow), lambda j: (0, j))
        pltpu.emit_pipeline(
            body,
            grid=(width // narrow,),
            in_specs=[
                pl.BlockSpec((n, part, width), lambda j: (0, 0, 0)),
                pl.BlockSpec((n * width, narrow), lambda j: (0, j)),
                strip,
            ],
            out_specs=[strip],
        )(blocks.at[:, here(c)], weight, fwd_add.at[here(c)], results.at[0, here(c)])

    def start_gather(c):
        for way in range(2):
            @pl.when((c < chunks) & (position(way) < n - 1))
            def _():
                gather_copy(way, 1, c).start()

    start_gather(0)

    @pl.loop(0, chunks + n - 1)
    def _(slot):
        start_gather(slot + 1)

        @pl.loop(1, n)
        def _(t):
            c = slot - t + 1

            @pl.loop(0, 2)
            def _(way):
                place = position(way)

                @pl.when((c >= 0) & (c < chunks) & (place <= t - 1))
                def _():
                    block = me + (1 - 2 * way) * (n - t)

                    @pl.when(place == 0)
                    def _():
                        first_sum(block, c)

                    @pl.when(place > 0)
                    def _():
                        sum_wait(way, t - 1, c)
                        later_sum(way, t, block, c)

                    sum_copy(way, t, c).start()

                d = slot - t

                @pl.when((d >= 0) & (d < chunks) & (place >= t))
                def _():
                    gather_wait(way, t, d)

                    @pl.when(place < n - 1)
                    def _():
                        gather_copy(way, t + 1, d).start()

        done = slot - (n - 1)

        @pl.when(done == 0)
        def _():
            own.wait()

        @pl.when(done >= 0)
        def _():
            base(done)
            relay_copy(0, done).start()
            for way in range(2):
                @pl.when(position(way) > 0)
                def _():
                    sum_wait(way, n - 1, done)
            last_sum(done)
            relay_copy(1, done).start()

    @pl.loop(0, chunks)
    def _(c):
        for way in range(2):
            @pl.when(position(way) < n - 1)
            def _():
                gather_copy(way, 1, c).wait_send()

            @pl.loop(1, n)
            def _(t):
                @pl.when((position(way) < n - 1) & (position(way) >= t - 1) & (t > 1))
                def _():
                    gather_copy(way, t, c).wait_send()

                @pl.when(position(way) <= t - 1)
                def _():
                    sum_copy(way, t, c).wait_send()
            relay_copy(way, c).wait_send()
            relay_copy(way, c).wait_recv()


def relay(h, g, weight, fwd_add, back_add, chunks):
    n = lax.axis_size("mp")
    rows, width = h.shape
    part = (rows, width)
    shapes = [part, part, (n,) + part, (2, n) + part, (n,) + part, (2,) + part]
    anywhere = pl.BlockSpec(memory_space=pl.ANY)
    dma = pltpu.SemaphoreType.DMA
    work = rows * weight.shape[0] * width * 4
    return pl.pallas_call(
        functools.partial(relay_kernel, n, chunks),
        out_shape=[jax.ShapeDtypeStruct(shape, jnp.bfloat16) for shape in shapes],
        in_specs=[anywhere] * 5,
        out_specs=[anywhere] * 6,
        scratch_shapes=[
            dma((2, n, chunks)), dma((2, n, chunks)),
            dma((2, n, chunks)), dma((2, n, chunks)),
            dma((2, chunks)), dma((2, chunks)), dma,
        ],
        compiler_params=pltpu.CompilerParams(
            collective_id=0, has_side_effects=True, vmem_limit_bytes=48 * 2**20
        ),
        cost_estimate=pl.CostEstimate(flops=work, bytes_accessed=10**9, transcendentals=0),
    )(h, g, weight, fwd_add, back_add)[:2]


def summed(value, axis):
    n = lax.axis_size(axis)
    if n > longest_line or n & (n - 1):
        return lax.psum(value, axis)
    step = 1
    while step < n:
        pairs = [(j, j ^ step) for j in range(n)]
        other = lax.ppermute(value.astype(jnp.bfloat16), axis, pairs)
        value = value + other.astype(jnp.float32)
        step *= 2
    return value


def dot(a, b, a_dim=1, b_dim=0):
    return lax.dot_general(
        a, b, (((a_dim,), (b_dim,)), ((), ())), preferred_element_type=jnp.float32
    )


def local(
    forward_input,
    stored_input,
    output_gradient,
    frozen_weight,
    adapter_down_factor,
    adapter_up_factor,
    adapter_index_list,
):
    f32, bf16 = jnp.float32, jnp.bfloat16
    h, x, g = forward_input[0], stored_input[0], output_gradient[0]
    weight = frozen_weight[0]
    n = lax.axis_size("mp")
    owners = lax.axis_size("adapter")
    core = lax.axis_index("adapter")
    held, rank, width = adapter_down_factor.shape[1:]
    rows = h.shape[0]
    seq_count = adapter_index_list.shape[2]
    seq_len = rows // seq_count
    def all_tables(table):
        flat = table.reshape(held * rank, width)
        return jnp.concatenate(
            [flat] + [shifted(flat, "adapter", -k) for k in range(1, owners)], axis=0
        )

    down_all = all_tables(adapter_down_factor[0])
    up_all = all_tables(adapter_up_factor[0])
    total = owners * held
    columns = total * rank

    def mask_of(ids):
        place = (ids - core * held + total) % total
        token_place = jnp.repeat(place, seq_len)
        owner = lax.broadcasted_iota(jnp.int32, (rows, columns), 1) // rank
        return token_place[:, None] == owner

    mask_fwd = mask_of(adapter_index_list[0, 0])
    mask_back = mask_of(adapter_index_list[1, 0])
    fold = (
        lax.broadcasted_iota(jnp.int32, (columns, rank), 0) % rank
        == lax.broadcasted_iota(jnp.int32, (columns, rank), 1)
    ).astype(bf16)

    def rank_product(values, table, mask):
        product = jnp.where(mask, dot(values, table, 1, 1), 0.0).astype(bf16)
        return dot(fold, product, 0, 1)

    def spread(code, mask):
        return jnp.where(mask, dot(code, fold, 0, 1), 0.0).astype(bf16)

    ranked = jnp.concatenate(
        [
            rank_product(h, down_all, mask_fwd),
            rank_product(x, down_all, mask_back),
            rank_product(g, up_all, mask_back),
        ],
        axis=1,
    )
    ranked = summed(ranked, "mp")
    u = spread(ranked[:, :rows].astype(bf16), mask_fwd)
    ub = spread(ranked[:, rows : 2 * rows].astype(bf16), mask_back)
    v = spread((adapter_scale * ranked[:, 2 * rows :]).astype(bf16), mask_back)

    def factor_gradient(code, values, scale):
        own = dot(code[:, : held * rank], values, 0, 0)
        for k in range(1, owners):
            theirs = dot(code[:, k * held * rank : (k + 1) * held * rank], values, 0, 0)
            own = own + shifted(theirs.astype(bf16), "adapter", k).astype(f32)
        return (own * scale).astype(bf16).reshape(held, rank, width)

    grad_a = factor_gradient(v, x, 1.0 / seq_len)
    grad_b = factor_gradient(ub, g, adapter_scale / seq_len)

    lora = dot(u, up_all).astype(bf16).astype(f32)
    fwd_add = h.astype(f32) + adapter_scale * lora
    back_add = g.astype(f32) + dot(v, down_all).astype(bf16).astype(f32)
    if n <= longest_line:
        fwd_next, back_next = relay(h, g, weight, fwd_add, back_add, chunk_count)
    else:
        base = dot(lax.all_gather(h, "mp", axis=1, tiled=True), weight)
        terms = dot(g, weight, 1, 1).astype(bf16)
        back = lax.psum_scatter(terms, "mp", scatter_dimension=1, tiled=True).astype(f32)
        fwd_next = shifted((fwd_add + base).astype(bf16), "section", 1)
        back_next = shifted((back_add + back).astype(bf16), "section", -1)
    return (fwd_next[None], back_next[None], grad_a[None], grad_b[None])


def solution(mesh):
    in_specs = (
        P("section", "adapter", "mp"),
        P("section", "adapter", "mp"),
        P("section", "adapter", "mp"),
        P("section", None, "mp"),
        P("section", "adapter", None, "mp"),
        P("section", "adapter", None, "mp"),
        P(None, "section", "adapter"),
    )
    out_specs = (
        P("section", "adapter", "mp"),
        P("section", "adapter", "mp"),
        P("section", "adapter", None, "mp"),
        P("section", "adapter", None, "mp"),
    )
    return jax.shard_map(local, mesh=mesh, in_specs=in_specs, out_specs=out_specs, check_vma=False)
```

time: 877 us -> 557 us (0.64); the launches traced: 864 us -> 555 us
  Pallas kernels: 0 us -> 448 us
  waiting for transfers between devices: 473 us -> 31.1 us
  matrix products: 249 us -> 62.3 us
  starting transfers between devices: 84.2 us -> 3.13 us
  local copies, waits for them, and re-layouts: 37.3 us -> 8.92 us
  other arithmetic: 19.6 us -> 0.94 us
    pallas_call x0 -> x1, Pallas kernels: none -> 448 us  [relay(): pl.pallas_call(functools.partial(relay_kernel, n, chunks), out_shape=[jax...]
    ppermute x24 -> x0, waiting for transfers between devices: 210 us -> none  [the longest x6 161 us: line_gather(): lax.ppermute(up[-1], axis, [(j, j + 1) for j in range(t - 1, n - 1)])]
    dot_general x30 -> x12, matrix products: 249 us -> 62.3 us  [dot(): lax.dot_general(a, b, (((a_dim,), (b_dim,)), ((), ())), preferred_element...]
    ppermute x8 -> x4, waiting for transfers between devices: 128 us -> 5.28 us  [shifted(): return lax.ppermute(value, axis, pairs)]
    ppermute x2, waiting for transfers between devices: 135 us -> 25.8 us  [summed(): other = lax.ppermute(value.astype(jnp.bfloat16), axis, pairs)]
    ppermute x24 -> x0, starting transfers between devices: 77 us -> none  [the longest x6 30.7 us: line_gather(): lax.ppermute(down[-1], axis, [(j, j - 1) for j in range(1, n - t + 1)])]
    unnamed x60 -> x28, local copies, waits for them, and re-layouts: 30.8 us -> 8.85 us
    convert_element_type x4 -> x0, other arithmetic: 12.5 us -> none  [the longest x2 7.07 us: line_scatter(): (second.astype(jnp.float32) + down.astype(jnp.float32)).astype(jnp.bfloat16)]
  transfers between devices with their start and end apart: 34 -> 6, of which waited for: 14 -> 3; matrix products, arithmetic and copies ran while one was open for 33% -> 8% of each run, Pallas kernels for 0% -> 81%
where the time goes in v2:
time: 557 us; the launch traced here: 555 us
  Pallas kernels  448 us (80%)
  matrix products  62.3 us (11%)
  waiting for transfers between devices  31.1 us (6%)
  local copies, waits for them, and re-layouts  8.92 us (2%)
    pallas_call x1, Pallas kernels, relay(): pl.pallas_call(functools.partial(relay_kernel, n, chunks), out_shape=[jax...  448 us
    dot_general x12, matrix products, dot(): lax.dot_general(a, b, (((a_dim,), (b_dim,)), ((), ())), preferred_element...  62.3 us
    ppermute x2, waiting for transfers between devices, summed(): other = lax.ppermute(value.astype(jnp.bfloat16), axis, pairs)  25.8 us
  transfers between devices with their start and end apart: 6, of which 3 were waited for; matrix products, arithmetic and copies ran while one was open for 8% of the time, Pallas kernels for 81%

profile of v2, /device:TPU:18, one launch (start us, length us, event | category | flops | bytes accessed | tf_op | source)
XLA Modules:
  0.0 554.7 jit_solution(12257902250746171075)
XLA Ops:
  1.2 0.7 and_select_fusion
  2.0 5.3 collective-permute-done
  7.3 1.3 copy-done.7
  8.6 8.7 %fusion.26 = f32[64,1024]{1,0:T(8,128)S(1)} fusion(bf16[1,1024,2048]{2,1,0:T(8,128)(2,1)} %param.8, s32[1024]{0:T(1024)S(1)} %get-tuple-element.12, s32[1024]{0:T(1024)S(1)} %get-tuple-element.14, s32[1024]{0:T(1024)S(1)} %get-tuple-element.17, pred[1024]{0:T(1024)(128)(4,1)S(1)} %get-tuple-element.19, bf16[512,2048]{1,0:T(8,128)(2,1)} %copy-done.7, ...), kind=kOutput, calls=%fused_computation.30 | convolution fusion | flops 4441964544 | bytes 8673280 | tf_op jit(solution)/shard_map/dot_general | solution.py:297
  17.3 7.9 %fusion.28 = f32[64,1024]{1,0:T(8,128)S(1)} fusion(s32[1024]{0:T(1024)S(1)} %get-tuple-element.14, s32[1024]{0:T(1024)S(1)} %get-tuple-element.17, s32[1024]{0:T(1024)S(1)} %get-tuple-element.13, pred[1024]{0:T(1024)(128)(4,1)S(1)} %get-tuple-element.19, bf16[512,2048]{1,0:T(8,128)(2,1)} %copy-done.7, bf16[512,2048]{1,0:T(8,128)(2,1)S(1)} %bitcast.65, ...), kind=kOutput, calls=%fused_computation.31 | convolution fusion | flops 4441964544 | bytes 8673280 | tf_op jit(solution)/shard_map/dot_general | solution.py:297
  25.2 8.8 %fusion.24 = f32[64,1024]{1,0:T(8,128)S(1)} fusion(bf16[512,2048]{1,0:T(8,128)(2,1)} %collective-permute-done.1, bf16[512,2048]{1,0:T(8,128)(2,1)} %bitcast.68, s32[1024]{0:T(1024)S(1)} %get-tuple-element.12, s32[1024]{0:T(1024)S(1)} %get-tuple-element.14, s32[1024]{0:T(1024)S(1)} %get-tuple-element.17, pred[1024]{0:T(1024)(128)(4,1)S(1)} %get-tuple-element.19, ...), kind=kOutput, calls=%fused_computation.29 | convolution fusion | flops 4441964544 | bytes 8673280 | tf_op jit(solution)/shard_map/dot_general | solution.py:297
  34.0 1.6 collective-permute-start.2
  35.7 9.6 %collective-permute-done.2 = bf16[64,3072]{1,0:T(8,128)(2,1)S(1)} collective-permute-done((bf16[64,3072]{1,0:T(8,128)(2,1)S(1)}, bf16[64,3072]{1,0:T(8,128)(2,1)S(1)}, u32[]{:S(2)}, u32[]{:S(2)}) %collective-permute-start.2) | collective-permute-done | bytes 393248 | tf_op jit(solution)/shard_map/ppermute | solution.py:290
  45.7 16.3 %collective-permute-done.3 = bf16[64,3072]{1,0:T(8,128)(2,1)S(1)} collective-permute-done((bf16[64,3072]{1,0:T(8,128)(2,1)S(1)}, bf16[64,3072]{1,0:T(8,128)(2,1)S(1)}, u32[]{:S(2)}, u32[]{:S(2)}) %collective-permute-start.3) | collective-permute-done | bytes 393248 | tf_op jit(solution)/shard_map/ppermute | solution.py:290
  62.1 1.2 fusion.7
  63.3 1.2 fusion.11
  64.5 1.2 fusion.10
  65.6 1.8 copy-done.2
  67.4 3.7 fusion.18
  71.1 3.7 convolution_convert_fusion
  74.9 0.5 collective-permute-start.5
  75.4 6.7 %convert_add_fusion.back_add = f32[1024,2048]{1,0:T(8,128)} fusion(bf16[1024,1024]{1,0:T(8,128)(2,1)S(1)} %fusion.10, bf16[512,2048]{1,0:T(8,128)(2,1)S(1)} %copy-done.8, bf16[512,2048]{1,0:T(8,128)(2,1)S(1)} %bitcast.66, bf16[1,1024,2048]{2,1,0:T(8,128)(2,1)S(1)} %copy-done.3), kind=kOutput, calls=%fused_computation | convolution fusion | flops 4311744512 | bytes 18874368 | tf_op jit(solution)/shard_map/dot_general | solution.py:297
  82.0 8.3 %multiply_add_fusion.fwd_add = f32[1024,2048]{1,0:T(8,128)} fusion(bf16[1024,1024]{1,0:T(8,128)(2,1)S(1)} %fusion.7, bf16[512,2048]{1,0:T(8,128)(2,1)} %collective-permute-done.1, bf16[512,2048]{1,0:T(8,128)(2,1)S(1)} %bitcast.69, bf16[1,1024,2048]{2,1,0:T(8,128)(2,1)S(1)} %copy-done.1), kind=kOutput, calls=%fused_computation.1 | convolution fusion | flops 4313841664 | bytes 18874368 | tf_op jit(solution)/shard_map/dot_general | solution.py:297
  90.3 447.5 %shard_map.102 = (bf16[1024,2048]{1,0:T(8,128)(2,1)S(1)}, bf16[1024,2048]{1,0:T(8,128)(2,1)}, bf16[4,1024,2048]{2,1,0:T(8,128)(2,1)}, bf16[2,4,1024,2048]{3,2,1,...) custom-call(bf16[1024,2048]{1,0:T(8,128)(2,1)} %bitcast.61, bf16[1024,2048]{1,0:T(8,128)(2,1)} %bitcast.62, ...), custom_call_target="tpu_custom_call" | custom-call | flops 68719476736 | bytes 1000000000 | tf_op jit(solution)/shard_map/pallas_call | solution.py:266
  537.9 5.6 %multiply_convert_fusion.1 = bf16[512,2048]{1,0:T(8,128)(2,1)} fusion(bf16[512,2048]{1,0:T(8,128)(2,1)} %collective-permute-done.4, bf16[1,1024,2048]{2,1,0:T(8,128)(2,1)S(1)} %copy-done.2, bf16[1024,1024]{1,0:T(8,128)(2,1)S(1)} %copy-done.12), kind=kOutput, calls=%fused_computation.25 | convolution fusion | flops 2151677952 | bytes 9437184 | tf_op jit(solution)/shard_map/dot_general | solution.py:297
  543.5 5.5 multiply_convert_fusion
  549.0 2.1 copy.13
  551.1 1.6 copy-done
  552.7 2.0 copy.14
  (37 shorter events, 1.4 us)
Async XLA Ops:
  0.6 6.6 %collective-permute-start = (bf16[512,2048]{1,0:T(8,128)(2,1)}, bf16[512,2048]{1,0:T(8,128)(2,1)S(1)}, u32[]{:S(2)}, u32[]{:S(2)}) collective-permute-start(bf16[512,2048]{1,0:T(8,128)(2,1)} %bitcast.63), channel_id=1, source_target_pairs={{0,4},{4,0},{1,5},{5,1},{2,6},{6,2},{3,7},{7,3},{8,12},{12,8},{9,1... | collective-permute-start | bytes 6291464 | tf_op jit(solution)/shard_map/ppermute | solution.py:18
  0.7 24.5 %collective-permute-start.1 = (bf16[512,2048]{1,0:T(8,128)(2,1)}, bf16[512,2048]{1,0:T(8,128)(2,1)}, u32[]{:S(2)}, u32[]{:S(2)}) collective-permute-start(bf16[512,2048]{1,0:T(8,128)(2,1)} %bitcast.67), channel_id=1, source_target_pairs={{0,4},{4,0},{1,5},{5,1},{2,6},{6,2},{3,7},{7,3},{8,12},{12,8},{9,1... | collective-permute-start | bytes 6291464 | tf_op jit(solution)/shard_map/ppermute | solution.py:18
  7.3 1.3 copy-start.7
  8.6 8.7 %copy-start.5 = (bf16[1,8,64,2048]{3,2,1,0:T(8,128)(2,1)S(1)}, bf16[1,8,64,2048]{3,2,1,0:T(8,128)(2,1)}, u32[]{:S(2)}) copy-start(bf16[1,8,64,2048]{3,2,1,0:T(8,128)(2,1)} %param.11) | copy-start | bytes 6291460
  34.0 11.2 %collective-permute-start.2 = (bf16[64,3072]{1,0:T(8,128)(2,1)S(1)}, bf16[64,3072]{1,0:T(8,128)(2,1)S(1)}, u32[]{:S(2)}, u32[]{:S(2)}) collective-permute-start(bf16[64,3072]{1,0:T(8,128)(2,1)S(1)} %fusion.40), channel_id=1, source_target_pairs={{0,1},{1,0},{2,3},{3,2},{4,5},{5,4},{6,7},{7,6},{8,9},{9,8},{10,11... | collective-permute-start | bytes 1179656 | tf_op jit(solution)/shard_map/ppermute | solution.py:290
  45.3 16.7 %collective-permute-start.3 = (bf16[64,3072]{1,0:T(8,128)(2,1)S(1)}, bf16[64,3072]{1,0:T(8,128)(2,1)S(1)}, u32[]{:S(2)}, u32[]{:S(2)}) collective-permute-start(bf16[64,3072]{1,0:T(8,128)(2,1)S(1)} %fusion.45), channel_id=1, source_target_pairs={{0,2},{1,3},{2,0},{3,1},{4,6},{5,7},{6,4},{7,5},{8,10},{9,11},{10,... | collective-permute-start | bytes 1179656 | tf_op jit(solution)/shard_map/ppermute | solution.py:290
  64.5 6.7 %copy-start.9 = (bf16[1024,1024]{1,0:T(8,128)(2,1)}, bf16[1024,1024]{1,0:T(8,128)(2,1)S(1)}, u32[]{:S(2)}) copy-start(bf16[1024,1024]{1,0:T(8,128)(2,1)S(1)} %fusion.11) | copy-start | bytes 6291460
  64.5 2.9 copy-start.2
  67.4 7.9 %copy-start.11 = (bf16[1024,1024]{1,0:T(8,128)(2,1)}, bf16[1024,1024]{1,0:T(8,128)(2,1)S(1)}, u32[]{:S(2)}) copy-start(bf16[1024,1024]{1,0:T(8,128)(2,1)S(1)} %fusion.10) | copy-start | bytes 6291460
  67.4 3.7 copy-start.3
  71.1 4.2 copy-start.8
  71.1 466.7 %collective-permute-start.4 = (bf16[512,2048]{1,0:T(8,128)(2,1)}, bf16[512,2048]{1,0:T(8,128)(2,1)}, u32[]{:S(2)}, u32[]{:S(2)}) collective-permute-start(bf16[512,2048]{1,0:T(8,128)(2,1)} %fusion.18), channel_id=1, source_target_pairs={{0,4},{4,0},{1,5},{5,1},{2,6},{6,2},{3,7},{7,3},{8,12},{12,8},{9,1... | collective-permute-start | bytes 6291464 | tf_op jit(solution)/shard_map/ppermute | solution.py:18
  74.9 7.2 %copy-start.1 = (bf16[1,1024,2048]{2,1,0:T(8,128)(2,1)S(1)}, bf16[1,1024,2048]{2,1,0:T(8,128)(2,1)}, u32[]{:S(2)}) copy-start(bf16[1,1024,2048]{2,1,0:T(8,128)(2,1)} %param.7) | copy-start | bytes 12582916
  74.9 7.2 %copy-start.6 = (bf16[1,8,64,2048]{3,2,1,0:T(8,128)(2,1)S(1)}, bf16[1,8,64,2048]{3,2,1,0:T(8,128)(2,1)}, u32[]{:S(2)}) copy-start(bf16[1,8,64,2048]{3,2,1,0:T(8,128)(2,1)} %param.12) | copy-start | bytes 6291460
  74.9 468.6 %collective-permute-start.5 = (bf16[512,2048]{1,0:T(8,128)(2,1)}, bf16[512,2048]{1,0:T(8,128)(2,1)}, u32[]{:S(2)}, u32[]{:S(2)}) collective-permute-start(bf16[512,2048]{1,0:T(8,128)(2,1)} %convolution_convert_fusion), channel_id=1, source_target_pairs={{0,4},{4,0},{1,5},{5,1},{2,6},{6,2},{3,7},{7,3},{8,12},{12,8},{9,1... | collective-permute-start | bytes 6291464 | tf_op jit(solution)/shard_map/ppermute | solution.py:18
  90.3 447.6 %copy-start.12 = (bf16[1024,1024]{1,0:T(8,128)(2,1)S(1)}, bf16[1024,1024]{1,0:T(8,128)(2,1)}, u32[]{:S(2)}) copy-start(bf16[1024,1024]{1,0:T(8,128)(2,1)} %copy-done.11) | copy-start | bytes 6291460
  537.9 5.6 %copy-start.4 = (bf16[1,1024,2048]{2,1,0:T(8,128)(2,1)S(1)}, bf16[1,1024,2048]{2,1,0:T(8,128)(2,1)}, u32[]{:S(2)}) copy-start(bf16[1,1024,2048]{2,1,0:T(8,128)(2,1)} %param.9) | copy-start | bytes 12582916
  537.9 5.6 %copy-start.10 = (bf16[1024,1024]{1,0:T(8,128)(2,1)S(1)}, bf16[1024,1024]{1,0:T(8,128)(2,1)}, u32[]{:S(2)}) copy-start(bf16[1024,1024]{1,0:T(8,128)(2,1)} %copy-done.9) | copy-start | bytes 6291460
  549.0 3.7 copy-start

commit v3 on v2

--- a/solution.py
+++ b/solution.py
@@ -19,9 +19,10 @@
 
 
 def relay_kernel(
-    n, chunks, h, g, weight, fwd_add, back_add,
-    fwd_next, back_next, blocks, arrived, sending, results,
+    n, chunks, h, g, weight, up_all, down_all, ranked, fold, mask_fwd, mask_back,
+    fwd_next, back_next, codes, blocks, arrived, sending, results,
     gather_send, gather_recv, sum_send, sum_recv, relay_send, relay_recv, own_sem,
+    rank_send, rank_recv, rank_parts, spread_fwd, spread_back,
 ):
     me = lax.axis_index("mp")
     section = lax.axis_index("section")
@@ -41,15 +42,35 @@
     for other in (after, before):
         pl.semaphore_signal(barrier, 1, device_id={"section": other}, device_id_type=mesh_id)
 
-    @pl.when(me > 0)
-    def _():
-        pl.semaphore_signal(barrier, 1, device_id={"mp": me - 1}, device_id_type=mesh_id)
-
-    @pl.when(me < n - 1)
-    def _():
-        pl.semaphore_signal(barrier, 1, device_id={"mp": me + 1}, device_id_type=mesh_id)
-
-    pl.semaphore_wait(barrier, 2 + (me > 0).astype(jnp.int32) + (me < n - 1).astype(jnp.int32))
+    for step in range(1, n):
+        peer = lax.rem(me + step, n)
+        pl.semaphore_signal(barrier, 1, device_id={"mp": peer}, device_id_type=mesh_id)
+    pl.semaphore_wait(barrier, n + 1)
+
+    def rank_copy(step):
+        return pltpu.make_async_remote_copy(
+            src_ref=ranked,
+            dst_ref=rank_parts.at[step - 1],
+            send_sem=rank_send.at[step - 1],
+            recv_sem=rank_recv.at[step - 1],
+            device_id={"mp": lax.rem(me + step, n)},
+            device_id_type=mesh_id,
+        )
+
+    for step in range(1, n):
+        rank_copy(step).start()
+
+    def sum_ranks():
+        total = ranked[...].astype(jnp.float32)
+        for step in range(1, n):
+            rank_copy(step).wait_recv()
+            total = total + rank_parts[step - 1].astype(jnp.float32)
+        codes[:, : 2 * rows] = total[:, : 2 * rows].astype(jnp.bfloat16)
+        codes[:, 2 * rows :] = (adapter_scale * total[:, 2 * rows :]).astype(jnp.bfloat16)
+
+    def spread_into(out, first, mask, c):
+        code = codes[:, pl.ds(pl.multiple_of(first * rows + c * part, part), part)]
+        out[...] = (dot(code, fold[...], 0, 1) * mask[here(c), :]).astype(jnp.bfloat16)
 
     own = pltpu.make_async_copy(h, blocks.at[me], own_sem)
     own.start()
@@ -137,26 +158,35 @@
         )(*refs, arrived.at[way, t - 1, here(c)], sending.at[block, here(c)])
 
     def last_sum(c):
-        def body(g_ref, w_ref, up_ref, down_ref, add_ref, out_ref):
-            total = dot(g_ref[...], w_ref[...], 1, 1) + add_ref[...]
+        spread_into(spread_back, 2, mask_back, c)
+
+        def body(g_ref, w_ref, up_ref, down_ref, add_ref, table_ref, out_ref):
+            total = dot(g_ref[...], w_ref[...], 1, 1) + add_ref[...].astype(jnp.float32)
+            term = dot(spread_back[...], table_ref[...]).astype(jnp.bfloat16)
+            total = total + term.astype(jnp.float32)
             up = jnp.where(me > 0, up_ref[...].astype(jnp.float32), 0.0)
             down = jnp.where(me < n - 1, down_ref[...].astype(jnp.float32), 0.0)
             out_ref[...] = (total + up + down).astype(jnp.bfloat16)
 
         specs, refs = product(me, c)
+        table = pl.BlockSpec((down_all.shape[0], tile), lambda j: (0, j))
         pltpu.emit_pipeline(
-            body, grid=(width // tile,), in_specs=specs + [piece] * 3, out_specs=[piece]
+            body, grid=(width // tile,), in_specs=specs + [piece] * 3 + [table], out_specs=[piece]
         )(
             *refs,
             arrived.at[0, n - 1, here(c)],
             arrived.at[1, n - 1, here(c)],
-            back_add.at[here(c)],
+            g.at[here(c)],
+            down_all,
             results.at[1, here(c)],
         )
 
     def base(c):
-        def body(b_ref, w_ref, add_ref, out_ref):
-            total = add_ref[...]
+        spread_into(spread_fwd, 0, mask_fwd, c)
+
+        def body(b_ref, w_ref, add_ref, table_ref, out_ref):
+            term = dot(spread_fwd[...], table_ref[...]).astype(jnp.bfloat16)
+            total = add_ref[...].astype(jnp.float32) + adapter_scale * term.astype(jnp.float32)
             for k in range(n):
                 total = total + dot(b_ref[k], w_ref[k * width : (k + 1) * width, :])
             out_ref[...] = total.astype(jnp.bfloat16)
@@ -169,9 +199,10 @@
                 pl.BlockSpec((n, part, width), lambda j: (0, 0, 0)),
                 pl.BlockSpec((n * width, narrow), lambda j: (0, j)),
                 strip,
+                pl.BlockSpec((up_all.shape[0], narrow), lambda j: (0, j)),
             ],
             out_specs=[strip],
-        )(blocks.at[:, here(c)], weight, fwd_add.at[here(c)], results.at[0, here(c)])
+        )(blocks.at[:, here(c)], weight, h.at[here(c)], up_all, results.at[0, here(c)])
 
     def start_gather(c):
         for way in range(2):
@@ -208,7 +239,7 @@
 
                     sum_copy(way, t, c).start()
 
-                d = slot - t
+                d = slot - t + 1
 
                 @pl.when((d >= 0) & (d < chunks) & (place >= t))
                 def _():
@@ -218,16 +249,22 @@
                     def _():
                         gather_copy(way, t + 1, d).start()
 
-        done = slot - (n - 1)
-
-        @pl.when(done == 0)
+        whole = slot - (n - 2)
+
+        @pl.when(whole == 0)
         def _():
             own.wait()
+            sum_ranks()
+
+        @pl.when((whole >= 0) & (whole < chunks))
+        def _():
+            base(whole)
+            relay_copy(0, whole).start()
+
+        done = slot - (n - 1)
 
         @pl.when(done >= 0)
         def _():
-            base(done)
-            relay_copy(0, done).start()
             for way in range(2):
                 @pl.when(position(way) > 0)
                 def _():
@@ -235,6 +272,9 @@
             last_sum(done)
             relay_copy(1, done).start()
 
+    for step in range(1, n):
+        rank_copy(step).wait_send()
+
     @pl.loop(0, chunks)
     def _(c):
         for way in range(2):
@@ -255,42 +295,35 @@
             relay_copy(way, c).wait_recv()
 
 
-def relay(h, g, weight, fwd_add, back_add, chunks):
+def relay(h, g, weight, up_all, down_all, ranked, fold, mask_fwd, mask_back, chunks):
     n = lax.axis_size("mp")
     rows, width = h.shape
     part = (rows, width)
-    shapes = [part, part, (n,) + part, (2, n) + part, (n,) + part, (2,) + part]
+    spread_shape = (rows // chunks, up_all.shape[0])
+    shapes = [part, part, ranked.shape, (n,) + part, (2, n) + part, (n,) + part, (2,) + part]
     anywhere = pl.BlockSpec(memory_space=pl.ANY)
+    inside = pl.BlockSpec(memory_space=pltpu.VMEM)
     dma = pltpu.SemaphoreType.DMA
     work = rows * weight.shape[0] * width * 4
     return pl.pallas_call(
         functools.partial(relay_kernel, n, chunks),
         out_shape=[jax.ShapeDtypeStruct(shape, jnp.bfloat16) for shape in shapes],
-        in_specs=[anywhere] * 5,
-        out_specs=[anywhere] * 6,
+        in_specs=[anywhere] * 5 + [inside] * 4,
+        out_specs=[anywhere] * 2 + [inside] + [anywhere] * 4,
         scratch_shapes=[
             dma((2, n, chunks)), dma((2, n, chunks)),
             dma((2, n, chunks)), dma((2, n, chunks)),
             dma((2, chunks)), dma((2, chunks)), dma,
+            dma((n - 1,)), dma((n - 1,)),
+            pltpu.VMEM((n - 1,) + ranked.shape, jnp.bfloat16),
+            pltpu.VMEM(spread_shape, jnp.bfloat16),
+            pltpu.VMEM(spread_shape, jnp.bfloat16),
         ],
         compiler_params=pltpu.CompilerParams(
-            collective_id=0, has_side_effects=True, vmem_limit_bytes=48 * 2**20
+            collective_id=0, has_side_effects=True, vmem_limit_bytes=56 * 2**20
         ),
         cost_estimate=pl.CostEstimate(flops=work, bytes_accessed=10**9, transcendentals=0),
-    )(h, g, weight, fwd_add, back_add)[:2]
-
-
-def summed(value, axis):
-    n = lax.axis_size(axis)
-    if n > longest_line or n & (n - 1):
-        return lax.psum(value, axis)
-    step = 1
-    while step < n:
-        pairs = [(j, j ^ step) for j in range(n)]
-        other = lax.ppermute(value.astype(jnp.bfloat16), axis, pairs)
-        value = value + other.astype(jnp.float32)
-        step *= 2
-    return value
+    )(h, g, weight, up_all, down_all, ranked, fold, mask_fwd, mask_back)[:3]
 
 
 def dot(a, b, a_dim=1, b_dim=0):
@@ -357,10 +390,18 @@
         ],
         axis=1,
     )
-    ranked = summed(ranked, "mp")
-    u = spread(ranked[:, :rows].astype(bf16), mask_fwd)
-    ub = spread(ranked[:, rows : 2 * rows].astype(bf16), mask_back)
-    v = spread((adapter_scale * ranked[:, 2 * rows :]).astype(bf16), mask_back)
+    if n <= longest_line:
+        fwd_next, back_next, codes = relay(
+            h, g, weight, up_all, down_all, ranked.astype(bf16), fold,
+            mask_fwd.astype(bf16), mask_back.astype(bf16), chunk_count,
+        )
+    else:
+        ranked = lax.psum(ranked, "mp")
+        codes = jnp.concatenate(
+            [ranked[:, : 2 * rows], adapter_scale * ranked[:, 2 * rows :]], axis=1
+        ).astype(bf16)
+    ub = spread(codes[:, rows : 2 * rows], mask_back)
+    v = spread(codes[:, 2 * rows :], mask_back)
 
     def factor_gradient(code, values, scale):
         own = dot(code[:, : held * rank], values, 0, 0)
@@ -372,12 +413,11 @@
     grad_a = factor_gradient(v, x, 1.0 / seq_len)
     grad_b = factor_gradient(ub, g, adapter_scale / seq_len)
 
-    lora = dot(u, up_all).astype(bf16).astype(f32)
-    fwd_add = h.astype(f32) + adapter_scale * lora
-    back_add = g.astype(f32) + dot(v, down_all).astype(bf16).astype(f32)
-    if n <= longest_line:
-        fwd_next, back_next = relay(h, g, weight, fwd_add, back_add, chunk_count)
-    else:
+    if n > longest_line:
+        u = spread(codes[:, :rows], mask_fwd)
+        lora = dot(u, up_all).astype(bf16).astype(f32)
+        fwd_add = h.astype(f32) + adapter_scale * lora
+        back_add = g.astype(f32) + dot(v, down_all).astype(bf16).astype(f32)
         base = dot(lax.all_gather(h, "mp", axis=1, tiled=True), weight)
         terms = dot(g, weight, 1, 1).astype(bf16)
         back = lax.psum_scatter(terms, "mp", scatter_dimension=1, tiled=True).astype(f32)

time: 557 us -> 529 us (0.950)
  waiting for transfers between devices: 31.1 us -> 0.01 us
  matrix products: 62.3 us -> 41.9 us
  Pallas kernels: 448 us -> 463 us
  other arithmetic: 0.94 us -> 14 us
    ppermute x2 -> x0, waiting for transfers between devices: 25.8 us -> none  [summed(): other = lax.ppermute(value.astype(jnp.bfloat16), axis, pairs)]
    dot_general x12 -> x9, matrix products: 62.3 us -> 41.9 us  [dot(): lax.dot_general(a, b, (((a_dim,), (b_dim,)), ((), ())), preferred_element...]
    pallas_call x1, Pallas kernels: 448 us -> 463 us  [relay(): pl.pallas_call(functools.partial(relay_kernel, n, chunks), out_shape=[jax...]
    concatenate x0 -> x3, other arithmetic: none -> 9.3 us  [the longest x2 8.5 us: all_tables(): jnp.concatenate([flat] + [shifted(flat, 'adapter', -k) for k in range(1,...]
  transfers between devices with their start and end apart: 6 -> 4, of which waited for: 3 -> 0; matrix products, arithmetic and copies ran while one was open for 8% -> 6% of each run, Pallas kernels for 81% -> 0%
where the time goes in v3:
time: 529 us; the launch traced here: 527 us
  Pallas kernels  463 us (88%)
  matrix products  41.9 us (8%)
  other arithmetic  14 us (3%)
  local copies, waits for them, and re-layouts  5.83 us (1%)
    pallas_call x1, Pallas kernels, relay(): pl.pallas_call(functools.partial(relay_kernel, n, chunks), out_shape=[jax...  463 us
    dot_general x9, matrix products, dot(): lax.dot_general(a, b, (((a_dim,), (b_dim,)), ((), ())), preferred_element...  41.9 us
  transfers between devices with their start and end apart: 4, of which 0 were waited for; matrix products, arithmetic and copies ran while one was open for 6% of the time, Pallas kernels for 0%

profile of v3, /device:TPU:18, one launch (start us, length us, event | category | flops | bytes accessed | tf_op | source)
XLA Modules:
  0.0 526.8 jit_solution(4615226869846428301)
XLA Ops:
  0.6 0.1 collective-permute-start.1
  0.7 0.5 collective-permute-start
  1.2 0.7 and_select_fusion.1
  2.0 0.1 broadcast_bitcast_fusion
  2.0 2.4 fusion.2
  4.5 1.5 fusion.44.fold
  6.0 7.9 %fusion.28 = bf16[64,1024]{1,0:T(8,128)(2,1)S(1)} fusion(s32[1024]{0:T(1024)S(1)} %get-tuple-element.16, s32[1024]{0:T(1024)S(1)} %get-tuple-element.19, s32[1024]{0:T(1024)S(1)} %get-tuple-element.15, pred[1024]{0:T(1024)(128)(4,1)S(1)} %get-tuple-element.20, s32[1024]{0:T(1024)S(1)} %get-tuple-element.17, s32[1024]{0:T(1024)S(1)} %get-tuple-element.18, ...), kind=kOutput, calls=%fused_computation.29 | convolution fusion | flops 4442030080 | bytes 8542208 | tf_op jit(solution)/shard_map/dot_general | solution.py:330
  13.9 7.9 %fusion.29 = bf16[64,1024]{1,0:T(8,128)(2,1)S(1)} fusion(bf16[1,1024,2048]{2,1,0:T(8,128)(2,1)} %param.8, s32[1024]{0:T(1024)S(1)} %get-tuple-element.14, s32[1024]{0:T(1024)S(1)} %get-tuple-element.16, s32[1024]{0:T(1024)S(1)} %get-tuple-element.19, pred[1024]{0:T(1024)(128)(4,1)S(1)} %get-tuple-element.20, s32[1024]{0:T(1024)S(1)} %get-tuple-element.17, ...), kind=kOutput, calls=%fused_computation.30 | convolution fusion | flops 4442030080 | bytes 8542208 | tf_op jit(solution)/shard_map/dot_general | solution.py:330
  21.8 8.8 %fusion.32 = bf16[64,1024]{1,0:T(8,128)(2,1)S(1)} fusion(s32[1024]{0:T(1024)S(1)} %get-tuple-element.14, s32[1024]{0:T(1024)S(1)} %get-tuple-element.16, s32[1024]{0:T(1024)S(1)} %get-tuple-element.19, pred[1024]{0:T(1024)(128)(4,1)S(1)} %get-tuple-element.20, s32[1024]{0:T(1024)S(1)} %get-tuple-element.17, s32[1024]{0:T(1024)S(1)} %get-tuple-element.18, ...), kind=kOutput, calls=%fused_computation.31 | convolution fusion | flops 4442030080 | bytes 8542208 | tf_op jit(solution)/shard_map/dot_general | solution.py:330
  30.6 0.8 pad_maximum_fusion.2.ranked
  31.4 4.3 pad_maximum_fusion.1.down_all
  35.7 4.2 pad_maximum_fusion.up_all
  39.9 463.3 %shard_map.102 = (bf16[1024,2048]{1,0:T(8,128)(2,1)}, bf16[1024,2048]{1,0:T(8,128)(2,1)}, bf16[64,3072]{1,0:T(8,128)(2,1)}, bf16[4,1024,2048]{2,1,0:T(8,128)(2,1...) custom-call(bf16[1024,2048]{1,0:T(8,128)(2,1)} %bitcast.72, ...), custom_call_target="tpu_custom_call" | custom-call | flops 68719476736 | bytes 1000000000 | tf_op jit(solution)/shard_map/pallas_call | solution.py:308
  503.2 2.2 fusion.11
  505.5 2.4 convolution_convert_fusion
  507.9 0.1 collective-permute-start.3
  508.0 2.2 fusion.10
  510.2 2.4 fusion.18
  512.7 0.4 collective-permute-start.2
  513.1 3.9 multiply_convert_fusion
  517.0 4.0 multiply_convert_fusion.1
  521.1 2.1 copy.13
  523.2 1.6 copy-done
  524.8 2.0 copy.14
  (18 shorter events, 0.1 us)
Async XLA Ops:
  0.6 5.3 %copy-start.2 = (bf16[1,8,64,2048]{3,2,1,0:T(8,128)(2,1)S(1)}, bf16[1,8,64,2048]{3,2,1,0:T(8,128)(2,1)}, u32[]{:S(2)}) copy-start(bf16[1,8,64,2048]{3,2,1,0:T(8,128)(2,1)} %param.11) | copy-start | bytes 6291460
  0.6 5.3 %collective-permute-start.1 = (bf16[512,2048]{1,0:T(8,128)(2,1)}, bf16[512,2048]{1,0:T(8,128)(2,1)}, u32[]{:S(2)}, u32[]{:S(2)}) collective-permute-start(bf16[512,2048]{1,0:T(8,128)(2,1)} %bitcast.64), channel_id=1, source_target_pairs={{0,4},{4,0},{1,5},{5,1},{2,6},{6,2},{3,7},{7,3},{8,12},{12,8},{9,1... | collective-permute-start | bytes 6291464 | tf_op jit(solution)/shard_map/ppermute | solution.py:18
  0.7 21.1 %collective-permute-start = (bf16[512,2048]{1,0:T(8,128)(2,1)}, bf16[512,2048]{1,0:T(8,128)(2,1)}, u32[]{:S(2)}, u32[]{:S(2)}) collective-permute-start(bf16[512,2048]{1,0:T(8,128)(2,1)} %bitcast.68), channel_id=1, source_target_pairs={{0,4},{4,0},{1,5},{5,1},{2,6},{6,2},{3,7},{7,3},{8,12},{12,8},{9,1... | collective-permute-start | bytes 6291464 | tf_op jit(solution)/shard_map/ppermute | solution.py:18
  31.4 4.3 copy-start.3
  503.2 2.3 copy-start.4
  507.9 2.3 copy-start.5
  507.9 5.2 collective-permute-start.3
  512.7 4.3 collective-permute-start.2
  517.0 4.0 copy-start.1
  521.1 3.7 copy-start
